TPU v7x, 32 devices: a whole 2x2x4 slice. The times are simulated.
32 devices in a mesh: dp: 8 (over y, x, core), tensor: 4 (over z).
Axes of the slice: x: 2, y: 2, z: 4, core: 2. Of those that a mesh axis runs over, the one named last changes fastest.
Arguments:
- tokens: bfloat16 [25216, 768], P('dp'), may hold values from -6 to 6
- cotangent: bfloat16 [25216, 768], P('dp'), may hold values from -6 to 6
- qkv_weight: float32 [3, 768, 768], P(None, 'dp', 'tensor'), may hold values from -0.21875 to 0.21875
- out_weight: float32 [768, 768], P('tensor', 'dp'), may hold values from -0.875 to 0.875
- up_weight: float32 [768, 3072], P('dp', 'tensor'), may hold values from -0.21875 to 0.21875
- down_weight: float32 [3072, 768], P('tensor', 'dp'), may hold values from -0.109375 to 0.109375
- shared_vectors: float32 [6, 768], P(None, 'dp'), may hold values from -0.5 to 1.4, as said below
- split_vectors: float32 [4, 1152], P('tensor', 'dp'), may hold values from -1.5 to 1.5
- qkv_first: float32 [3, 768, 768], P(None, 'dp', 'tensor'), may hold values from -80 to 80
- qkv_second: float32 [3, 768, 768], P(None, 'dp', 'tensor'), may hold values from 6.304 to 100.864
- out_first: float32 [768, 768], P('tensor', 'dp'), may hold values from -16 to 16
- out_second: float32 [768, 768], P('tensor', 'dp'), may hold values from 0.25216 to 4.03456
- up_first: float32 [768, 3072], P('dp', 'tensor'), may hold values from -32 to 32
- up_second: float32 [768, 3072], P('dp', 'tensor'), may hold values from 1.13472 to 18.15552
- down_first: float32 [3072, 768], P('tensor', 'dp'), may hold values from -64 to 64
- down_second: float32 [3072, 768], P('tensor', 'dp'), may hold values from 4.53888 to 73.1264
- shared_first: float32 [6, 768], P(None, 'dp'), may hold values from -80 to 80
- shared_second: float32 [6, 768], P(None, 'dp'), may hold values from 6.304 to 100.864
- split_first: float32 [4, 1152], P('tensor', 'dp'), may hold values from -80 to 80
- split_second: float32 [4, 1152], P('tensor', 'dp'), may hold values from 6.304 to 100.864
Outputs:
- block_out: bfloat16 [25216, 768], P('dp')
- tokens_grad: bfloat16 [25216, 768], P('dp')
- qkv_first_new: float32 [3, 768, 768], P(None, 'dp', 'tensor')
- qkv_second_new: float32 [3, 768, 768], P(None, 'dp', 'tensor')
- qkv_updated: float32 [3, 768, 768], P(None, 'dp', 'tensor')
- out_first_new: float32 [768, 768], P('tensor', 'dp')
- out_second_new: float32 [768, 768], P('tensor', 'dp')
- out_updated: float32 [768, 768], P('tensor', 'dp')
- up_first_new: float32 [768, 3072], P('dp', 'tensor')
- up_second_new: float32 [768, 3072], P('dp', 'tensor')
- up_updated: float32 [768, 3072], P('dp', 'tensor')
- down_first_new: float32 [3072, 768], P('tensor', 'dp')
- down_second_new: float32 [3072, 768], P('tensor', 'dp')
- down_updated: float32 [3072, 768], P('tensor', 'dp')
- shared_first_new: float32 [6, 768], P(None, 'dp')
- shared_second_new: float32 [6, 768], P(None, 'dp')
- shared_updated: float32 [6, 768], P(None, 'dp')
- split_first_new: float32 [4, 1152], P('tensor', 'dp')
- split_second_new: float32 [4, 1152], P('tensor', 'dp')
- split_updated: float32 [4, 1152], P('tensor', 'dp')
Inputs may be any that keep to these rules, and one draw needn't show every extreme that they name: `shared_vectors`: rows 0 and 2 lie in 0.6 to 1.4, the other rows in -0.5 to 0.5.
All inputs are finite; a program needn't handle non-finite values.
Results may differ from a plain program's by a relative error of at most 0.025.
Values may be sent and summed in bfloat16 or wider, within the bound.
A program may use at most 192 MiB of HBM per device.

v0:
```python
from functools import partial
import math

import jax
import jax.numpy as jnp
from jax import lax
from jax.sharding import PartitionSpec as P

HEAD = 64
SEQ = 197
STEP = 10


EPS_NORM = 1e-06
EPS_ADAM = 1e-08
BETA_ONE = 0.9
BETA_TWO = 0.999
RATE_MATRIX = 0.05
RATE_VECTOR = 0.2
DECAY_MATRIX = 0.05


def contract_rows(left, right):
    return lax.dot_general(
        left, right, (((0,), (0,)), ((), ())), preferred_element_type=jnp.float32
    )


def contract_cols(left, right):
    return lax.dot_general(
        left, right, (((1,), (1,)), ((), ())), preferred_element_type=jnp.float32
    )


def norm_parts(values):
    centre = values - jnp.mean(values, axis=-1, keepdims=True)
    factor = lax.rsqrt(jnp.mean(centre * centre, axis=-1, keepdims=True) + EPS_NORM)
    return (centre * factor, factor)


def norm_backward(grad_out, unit, factor, gain):
    scaled = grad_out * gain
    inner = (
        scaled
        - jnp.mean(scaled, axis=-1, keepdims=True)
        - unit * jnp.mean(scaled * unit, axis=-1, keepdims=True)
    )
    return (inner * factor, jnp.sum(grad_out * unit, axis=0), jnp.sum(grad_out, axis=0))


def adam_step(weight, gradient, first, second, rate, decay):
    first = BETA_ONE * first + (1.0 - BETA_ONE) * gradient
    second = BETA_TWO * second + (1.0 - BETA_TWO) * gradient * gradient
    corr_one = 1.0 - BETA_ONE**STEP
    corr_two = 1.0 - BETA_TWO**STEP
    updated = weight * (1.0 - rate * decay) - rate * (first / corr_one) / (
        jnp.sqrt(second / corr_two) + EPS_ADAM
    )
    return (first, second, updated)


def per_device(
    tokens,
    cotangent,
    qkv_weight,
    out_weight,
    up_weight,
    down_weight,
    shared_vectors,
    split_vectors,
    qkv_first,
    qkv_second,
    out_first,
    out_second,
    up_first,
    up_second,
    down_first,
    down_second,
    shared_first,
    shared_second,
    split_first,
    split_second,
):
    low_type = jnp.bfloat16
    qkv_full, out_full, up_full, down_full = (
        lax.all_gather(qkv_weight.astype(low_type), "dp", axis=1, tiled=True),
        lax.all_gather(out_weight.astype(low_type), "dp", axis=1, tiled=True),
        lax.all_gather(up_weight.astype(low_type), "dp", axis=0, tiled=True),
        lax.all_gather(down_weight.astype(low_type), "dp", axis=1, tiled=True),
    )
    shared_full, split_full = (
        lax.all_gather(shared_vectors, "dp", axis=1, tiled=True),
        lax.all_gather(split_vectors, "dp", axis=1, tiled=True),
    )
    row_count = tokens.shape[0]
    images = row_count // SEQ
    local_width = qkv_full.shape[2]
    head_count = local_width // HEAD
    bias_table = split_full[0].reshape(local_width, 6)
    query_bias = bias_table[:, 0]
    value_bias = bias_table[:, 1]
    hidden_bias = bias_table[:, 2:].reshape(-1)
    score_scale = 1.0 / math.sqrt(HEAD)
    head_shape = (images, SEQ, head_count, HEAD)
    inputs = tokens.astype(jnp.float32)
    back_rows = cotangent.astype(jnp.float32)
    unit_one, factor_one = norm_parts(inputs)
    normed = (unit_one * shared_full[0] + shared_full[1]).astype(low_type)
    projected = jnp.einsum("td,cde->cte", normed, qkv_full, preferred_element_type=jnp.float32)
    queries = (projected[0] + query_bias).astype(low_type).reshape(head_shape)
    key_heads = projected[1].astype(low_type).reshape(head_shape)
    value_heads = (projected[2] + value_bias).astype(low_type).reshape(head_shape)
    scores = (
        jnp.einsum("bqhe,bkhe->bhqk", queries, key_heads, preferred_element_type=jnp.float32)
        * score_scale
    )
    highest = jnp.max(scores, axis=-1, keepdims=True)
    exponent = jnp.exp(scores - highest)
    row_total = jnp.sum(exponent, axis=-1, keepdims=True)
    log_total = highest + jnp.log(row_total)
    probs_low = (exponent / row_total).astype(low_type)
    attended = jnp.einsum(
        "bhqk,bkhe->bqhe", probs_low, value_heads, preferred_element_type=jnp.float32
    )
    attended = attended.reshape(row_count, local_width).astype(low_type)
    branch_terms = jnp.dot(attended, out_full, preferred_element_type=jnp.float32)
    branch = lax.psum(branch_terms.astype(jnp.bfloat16), "tensor").astype(jnp.float32)
    middle = inputs + branch + shared_full[4]
    unit_two, factor_two = norm_parts(middle)
    normed_two_part = (unit_two * shared_full[2] + shared_full[3]).astype(low_type)
    hidden_in = jnp.dot(normed_two_part, up_full, preferred_element_type=jnp.float32) + hidden_bias
    gelu_value, gelu_pull = jax.vjp(partial(jax.nn.gelu, approximate=False), hidden_in)
    hidden = gelu_value.astype(low_type)
    feed_terms = jnp.dot(hidden, down_full, preferred_element_type=jnp.float32)
    feed = lax.psum(feed_terms.astype(jnp.bfloat16), "tensor").astype(jnp.float32)
    out_part = (middle + feed + shared_full[5]).astype(low_type)
    down_grad = contract_rows(hidden, cotangent)
    hidden_back = contract_cols(cotangent, down_full)
    hidden_in_back = gelu_pull(hidden_back)[0].astype(low_type)
    up_grad = contract_rows(normed_two_part, hidden_in_back)
    hidden_bias_grad = jnp.sum(hidden_in_back.astype(jnp.float32), axis=0)
    normed_two_terms = contract_cols(hidden_in_back, up_full)
    normed_two_back = lax.psum(normed_two_terms.astype(jnp.bfloat16), "tensor").astype(jnp.float32)
    middle_part, gain_two_grad, shift_two_grad = norm_backward(
        normed_two_back, unit_two, factor_two, shared_full[2]
    )
    middle_back = back_rows + middle_part
    branch_back = middle_back.astype(low_type)
    out_grad = contract_rows(attended, branch_back)
    attended_back = contract_cols(branch_back, out_full).astype(low_type).reshape(head_shape)
    again = (
        jnp.einsum("bqhe,bkhe->bhqk", queries, key_heads, preferred_element_type=jnp.float32)
        * score_scale
    )
    probs_full = jnp.exp(again - log_total)
    probs_again = probs_full.astype(low_type)
    value_back = jnp.einsum(
        "bhqk,bqhe->bkhe", probs_again, attended_back, preferred_element_type=jnp.float32
    ).astype(low_type)
    probs_back = jnp.einsum(
        "bqhe,bkhe->bhqk", attended_back, value_heads, preferred_element_type=jnp.float32
    )
    weighted = jnp.sum(probs_full * probs_back, axis=-1, keepdims=True)
    scores_back = (probs_full * (probs_back - weighted) * score_scale).astype(low_type)
    query_back = jnp.einsum(
        "bhqk,bkhe->bqhe", scores_back, key_heads, preferred_element_type=jnp.float32
    ).astype(low_type)
    key_back = jnp.einsum(
        "bhqk,bqhe->bkhe", scores_back, queries, preferred_element_type=jnp.float32
    ).astype(low_type)
    projected_back = jnp.stack([query_back, key_back, value_back]).reshape(
        3, row_count, local_width
    )
    qkv_grad = jnp.einsum("td,cte->cde", normed, projected_back, preferred_element_type=jnp.float32)
    query_bias_grad = jnp.sum(projected_back[0].astype(jnp.float32), axis=0)
    value_bias_grad = jnp.sum(projected_back[2].astype(jnp.float32), axis=0)
    normed_terms = jnp.einsum(
        "cte,cde->td", projected_back, qkv_full, preferred_element_type=jnp.float32
    )
    normed_back = lax.psum(normed_terms.astype(jnp.bfloat16), "tensor").astype(jnp.float32)
    input_part, gain_one_grad, shift_one_grad = norm_backward(
        normed_back, unit_one, factor_one, shared_full[0]
    )
    grad_part = (middle_back + input_part).astype(low_type)
    shared_grad = jnp.stack(
        [
            gain_one_grad,
            shift_one_grad,
            gain_two_grad,
            shift_two_grad,
            jnp.sum(middle_back, axis=0),
            jnp.sum(back_rows, axis=0),
        ]
    )
    split_grad = jnp.concatenate(
        [
            query_bias_grad[:, None],
            value_bias_grad[:, None],
            hidden_bias_grad.reshape(local_width, -1),
        ],
        axis=1,
    ).reshape(1, -1)
    qkv_sum, out_sum, up_sum, down_sum, shared_sum, split_sum = (
        lax.psum_scatter(
            qkv_grad.astype(jnp.bfloat16), "dp", scatter_dimension=1, tiled=True
        ).astype(jnp.float32),
        lax.psum_scatter(
            out_grad.astype(jnp.bfloat16), "dp", scatter_dimension=1, tiled=True
        ).astype(jnp.float32),
        lax.psum_scatter(
            up_grad.astype(jnp.bfloat16), "dp", scatter_dimension=0, tiled=True
        ).astype(jnp.float32),
        lax.psum_scatter(
            down_grad.astype(jnp.bfloat16), "dp", scatter_dimension=1, tiled=True
        ).astype(jnp.float32),
        lax.psum_scatter(
            shared_grad.astype(jnp.bfloat16), "dp", scatter_dimension=1, tiled=True
        ).astype(jnp.float32),
        lax.psum_scatter(
            split_grad.astype(jnp.bfloat16), "dp", scatter_dimension=1, tiled=True
        ).astype(jnp.float32),
    )
    qkv_new = adam_step(qkv_weight, qkv_sum, qkv_first, qkv_second, RATE_MATRIX, DECAY_MATRIX)
    out_new = adam_step(out_weight, out_sum, out_first, out_second, RATE_MATRIX, DECAY_MATRIX)
    up_new = adam_step(up_weight, up_sum, up_first, up_second, RATE_MATRIX, DECAY_MATRIX)
    down_new = adam_step(down_weight, down_sum, down_first, down_second, RATE_MATRIX, DECAY_MATRIX)
    shared_new = adam_step(
        shared_vectors, shared_sum, shared_first, shared_second, RATE_VECTOR, 0.0
    )
    split_new = adam_step(split_vectors, split_sum, split_first, split_second, RATE_VECTOR, 0.0)
    return (
        out_part,
        grad_part,
        qkv_new[0],
        qkv_new[1],
        qkv_new[2],
        out_new[0],
        out_new[1],
        out_new[2],
        up_new[0],
        up_new[1],
        up_new[2],
        down_new[0],
        down_new[1],
        down_new[2],
        shared_new[0],
        shared_new[1],
        shared_new[2],
        split_new[0],
        split_new[1],
        split_new[2],
    )


def solution(mesh):
    placed = (
        P("dp", None),
        P("dp", None),
        P(None, "dp", "tensor"),
        P("tensor", "dp"),
        P("dp", "tensor"),
        P("tensor", "dp"),
        P(None, "dp"),
        P("tensor", "dp"),
        P(None, "dp", "tensor"),
        P(None, "dp", "tensor"),
        P("tensor", "dp"),
        P("tensor", "dp"),
        P("dp", "tensor"),
        P("dp", "tensor"),
        P("tensor", "dp"),
        P("tensor", "dp"),
        P(None, "dp"),
        P(None, "dp"),
        P("tensor", "dp"),
        P("tensor", "dp"),
    )
    return jax.shard_map(
        per_device,
        mesh=mesh,
        in_specs=placed,
        out_specs=(
            P("dp", None),
            P("dp", None),
            P(None, "dp", "tensor"),
            P(None, "dp", "tensor"),
            P(None, "dp", "tensor"),
            P("tensor", "dp"),
            P("tensor", "dp"),
            P("tensor", "dp"),
            P("dp", "tensor"),
            P("dp", "tensor"),
            P("dp", "tensor"),
            P("tensor", "dp"),
            P("tensor", "dp"),
            P("tensor", "dp"),
            P(None, "dp"),
            P(None, "dp"),
            P(None, "dp"),
            P("tensor", "dp"),
            P("tensor", "dp"),
            P("tensor", "dp"),
        ),
        check_vma=False,
    )
```

profile of v0, /device:TPU:0, one launch (start us, length us, event | category | flops | bytes accessed | tf_op | source)
XLA Modules:
  0.0 1049.0 jit_solution(517032689993775206)
XLA Ops:
  8.1 3.1 convert_reduce_fusion
  11.2 3.9 fusion.18
  15.2 10.5 %all-gather = f32[8,96,6]{1,2,0:T(8,128)S(1)} all-gather(f32[1,96,6]{1,2,0:T(8,128)S(1)} %bitcast.100), channel_id=1, replica_groups=mesh['dp'=8,'tensor'=4] {'dp'}, dimensions={0}, use_global_device_ids=true | all-gather | bytes 20736 | tf_op jit(solution)/shard_map/all_gather | solution.py:92
  26.6 13.4 %all_gather.19 = bf16[3,768,192]{2,0,1:T(4,128)(2,1)S(1)} all-gather(bf16[3,96,192]{2,0,1:T(4,128)(2,1)S(1)} %copy.163), channel_id=1, replica_groups=mesh['dp'=8,'tensor'=4] {'dp'}, dimensions={1}, use_global_device_ids=true | all-gather | bytes 995328 | tf_op jit(solution)/shard_map/all_gather | solution.py:86
  40.8 6.2 fusion.123
  51.5 13.4 %all-reduce = f32[1152]{0:T(1024)S(1)} all-reduce(f32[1152]{0:T(1024)S(1)} %dynamic-update-slice), channel_id=1, replica_groups=mesh['dp'=8,'tensor'=4] {'dp'}, use_global_device_ids=true, to_apply=%add | all-reduce | flops 1152 | bytes 9216
  66.2 8.8 all_gather.21
  75.0 6.8 convert_element_type.179
  81.8 5.7 squeeze.4
  87.5 5.7 squeeze.10
  93.3 6.6 multiply_reduce_fusion.2
  102.0 4.1 fusion.77
  107.0 2.4 convert_element_type.183
  110.5 3.8 convolution_convert_fusion.2
  116.1 174.7 %all-reduce.6.cloned.1.call-done = bf16[3152,768]{1,0:T(8,128)(2,1)} async-done(((bf16[3152,768]{1,0:T(8,128)(2,1)}), bf16[3152,768]{1,0:T(8,128)(2,1)}) %all-reduce.6.cloned.1.call-update) | async-done | bytes 4841488 | tf_op jit(solution)/shard_map/psum | solution.py:127
  290.8 5.6 fusion.60
  299.7 4.6 add_convert_fusion.2
  304.3 10.4 fusion.145
  314.6 29.0 %fusion.126 = (bf16[768]{0:T(1024)(128)(2,1)S(1)}, bf16[3152,768]{1,0:T(8,128)(2,1)S(1)}, f32[3152,768]{1,0:T(8,128)}) fusion(f32[3152,768]{1,0:T(8,128)} %fusion.145, f32[768]{0:T(1024)S(1)} %add.218, bf16[3152,768]{1,0:T(8,128)(2,1)} %param.21, bf16[768,768]{0,1:T(8,128)(2,1)} %all-gather.6.cloned.1.call-done), kind=kOutput, calls=%fused_computation.165 | convolution fusion | flops 3897384192 | bytes 30233088 | tf_op jit(solution)/shard_map/dot_general | solution.py:30
  345.8 5.8 convolution_convert_fusion
  351.9 9.1 convolution_convert_fusion.5
  361.1 10.4 multiply_convert_fusion.1
  371.6 9.2 convolution_convert_fusion.4
  381.3 145.5 %all-reduce.8.cloned.1.call-done = bf16[3152,768]{1,0:T(8,128)(2,1)} async-done(((bf16[3152,768]{1,0:T(8,128)(2,1)}), bf16[3152,768]{1,0:T(8,128)(2,1)}) %all-reduce.8.cloned.1.call-update) | async-done | bytes 4841488 | tf_op jit(solution)/shard_map/psum | solution.py:143
  526.8 9.4 fusion.23
  536.2 8.9 fusion.130
  545.1 3.7 copy-done.1
  550.5 4.8 reshape.153
  555.2 6.2 fusion.141
  561.6 9.2 fusion.88
  570.8 17.2 %fusion.142 = (bf16[3,64]{1,0:T(4,128)(2,1)S(1)}, bf16[16,197,3,64]{1,3,2,0:T(8,128)(2,1)}) fusion(f32[16,3,197,197]{2,3,1,0:T(8,128)} %fusion.88, f32[16,3,197,197]{2,3,1,0:T(8,128)} %copy-done.2, f32[16,3,197]{2,1,0:T(4,128)S(1)} %log_add_fusion, bf16[16,197,3,64]{1,0,3,2:T(8,128)(2,1)} %convert_element_type.179), kind=kOutput, calls=%fused_computation.169 | convolution fusion | flops 256427808 | bytes 17361600 | tf_op jit(solution)/shard_map/bhqk,bkhe->bqhe/dot_general | solution.py:165
  589.2 3.5 copy.174
  592.7 4.3 stack.40
  599.4 4.9 fusion.96
  604.4 19.6 %fusion.78 = bf16[16,197,3,64]{1,3,2,0:T(8,128)(2,1)} fusion(f32[16,3,197,197]{2,3,1,0:T(8,128)} %fusion.88, f32[16,3,197,197]{2,3,1,0:T(8,128)} %copy-done.2, f32[16,3,197]{2,1,0:T(4,128)S(1)} %log_add_fusion, f32[16,197,3,64]{1,0,3,2:T(8,128)} %copy-done.6, f32[3,64]{1,0:T(4,128)S(1)} %copy-done.45), kind=kOutput, calls=%fused_computation.97 | convolution fusion | flops 257033184 | bytes 18572352 | tf_op jit(solution)/shard_map/bhqk,bqhe->bkhe/dot_general | solution.py:168
  625.9 2.4 stack.42
  630.6 3.2 stack.41
  637.5 6.9 fusion.93
  647.9 9.2 convolution_convert_fusion.1
  657.1 5.8 bitcast_convert_fusion
  664.0 3.1 reduce.8
  671.5 3.1 reduce.7
  677.8 34.3 %reduce-scatter.19.cloned.1.call-done = bf16[96,576]{1,0:T(8,128)(2,1)} async-done(((bf16[768,576]{1,0:T(8,128)(2,1)}), bf16[96,576]{1,0:T(8,128)(2,1)}) %reduce-scatter.19.cloned.1.call-update) | async-done | bytes 110608
  716.2 279.4 %all-reduce.10.cloned.1.call-done = (bf16[3152,768]{1,0:T(8,128)(2,1)}, bf16[3152,768]{1,0:T(8,128)(2,1)}) async-done(((bf16[3152,768]{1,0:T(8,128)(2,1)}, bf16[3152,768]{1,0:T(8,128)(2,1)}), (bf16[3152,768]{1,0:T(8,128)(2,1)}, bf16[3152,768]{1,0:T(8,128)(2,1)})) %all-reduce.10.cloned.1.call-update) | async-done | bytes 9682960 | tf_op jit(solution)/shard_map/psum | solution.py:135
  995.6 3.1 reduce.6
  998.7 7.5 fusion.25
  1007.3 15.9 %fusion.17 = (bf16[3152,768]{1,0:T(8,128)(2,1)}, bf16[3152,768]{1,0:T(8,128)(2,1)}) fusion(f32[3152,768]{1,0:T(8,128)} %copy-done.1, bf16[3152,768]{1,0:T(8,128)(2,1)} %param.20, bf16[3152,768]{1,0:T(8,128)(2,1)} %get-tuple-element.155, f32[3152]{0:T(1024)S(1)} %broadcast_multiply_fusion, f32[3152]{0:T(1024)S(1)} %broadcast_multiply_fusion.1, ...), kind=kLoop, calls=%fused_computation.30 | loop fusion | flops 43573248 | bytes 38791424 | tf_op jit(solution)/shard_map/convert_element_type | solution.py:184
  1023.2 16.7 %reduce-scatter.23.cloned.1.call-done = bf16[96,6]{1,0:T(8,128)(2,1)} async-done(((bf16[768,6]{1,0:T(8,128)(2,1)}), bf16[96,6]{1,0:T(8,128)(2,1)}) %reduce-scatter.23.cloned.1.call-update) | async-done | bytes 1168
  (220 shorter events, 50.6 us)
Async XLA Ops:
  8.0 7.1 copy-start.42
  8.0 18.4 %copy-start.12 = (f32[3,96,192]{2,1,0:T(8,128)S(1)}, f32[3,96,192]{2,1,0:T(8,128)}, u32[]{:S(2)}) copy-start(f32[3,96,192]{2,1,0:T(8,128)} %param.22) | copy-start | bytes 663556
  8.0 282.7 %all-reduce.6.cloned.1.call-start = ((), (), s32[]{:S(2)}) async-start(), calls=%async_computation.6 | async-start | bytes 9682944 | tf_op jit(solution)/shard_map/psum | solution.py:127
  11.2 29.6 %copy-start.31 = (f32[3152]{0:T(1024)}, f32[3152]{0:T(1024)S(1)}, u32[]{:S(2)}) copy-start(f32[3152]{0:T(1024)S(1)} %broadcast_multiply_fusion.5) | copy-start | bytes 37828
  15.1 25.7 %copy-start.35 = (f32[3152]{0:T(1024)}, f32[3152]{0:T(1024)S(1)}, u32[]{:S(2)}) copy-start(f32[3152]{0:T(1024)S(1)} %add_rsqrt_fusion.1) | copy-start | bytes 37828
  26.4 14.4 %copy-start.39 = (f32[768]{0:T(1024)}, f32[768]{0:T(1024)S(1)}, u32[]{:S(2)}) copy-start(f32[768]{0:T(1024)S(1)} %get-tuple-element.153) | copy-start | bytes 9220
  26.4 14.4 %copy-start.52 = (f32[768]{0:T(1024)}, f32[768]{0:T(1024)S(1)}, u32[]{:S(2)}) copy-start(f32[768]{0:T(1024)S(1)} %get-tuple-element.152) | copy-start | bytes 9220
  47.1 17.9 %copy-start.23 = (f32[192,96]{1,0:T(8,128)S(1)}, f32[192,96]{1,0:T(8,128)}, u32[]{:S(2)}) copy-start(f32[192,96]{1,0:T(8,128)} %param.23) | copy-start | bytes 221188
  65.2 22.3 %copy-start.10 = (f32[192,6]{1,0:T(8,128)}, f32[192,6]{1,0:T(8,128)S(1)}, u32[]{:S(2)}) copy-start(f32[192,6]{1,0:T(8,128)S(1)} %reshape_squeeze.3) | copy-start | bytes 13828
  66.2 33.7 %copy-start.44 = (f32[3,64]{1,0:T(4,128)}, f32[3,64]{1,0:T(4,128)S(1)}, u32[]{:S(2)}) copy-start(f32[3,64]{1,0:T(4,128)S(1)} %add.207) | copy-start | bytes 2308
  75.0 34.4 %copy-start.8 = (bf16[192,768]{0,1:T(8,128)(2,1)}, bf16[192,768]{0,1:T(8,128)(2,1)S(1)}, u32[]{:S(2)}) copy-start(bf16[192,768]{0,1:T(8,128)(2,1)S(1)} %all_gather.21) | copy-start | bytes 884740
  93.3 8.7 copy-start.6
  93.3 8.7 copy-start.7
  93.3 8.7 copy-start.46
  107.0 8.8 copy-start.11
  114.3 182.2 %slice-start = ((s8[4841472]{0:T(1024)(128)(4,1)}), s8[647168]{0:T(1024)(128)(4,1)S(1)}, s32[]{:S(2)}) async-start(s8[4841472]{0:T(1024)(128)(4,1)} %bitcast.86), calls=%async_computation.17 | async-start | bytes 1294336
  114.3 190.0 %all-gather.4.cloned.1.call-start = ((), (), s32[]{:S(2)}) async-start(), calls=%async_computation.7 | async-start | bytes 1327104 | tf_op jit(solution)/shard_map/all_gather | solution.py:88
  115.1 199.6 %all-gather.6.cloned.1.call-start = ((), (), s32[]{:S(2)}) async-start(), calls=%async_computation.8 | async-start | bytes 1327104 | tf_op jit(solution)/shard_map/all_gather | solution.py:89
  115.8 411.0 %all-reduce.8.cloned.1.call-start = ((), (), s32[]{:S(2)}) async-start(), calls=%async_computation.9 | async-start | bytes 9682944 | tf_op jit(solution)/shard_map/psum | solution.py:143
  314.6 31.2 %copy-start.56 = (bf16[768,768]{1,0:T(8,128)(2,1)S(1)}, bf16[768,768]{1,0:T(8,128)(2,1)}, u32[]{:S(2)}) copy-start(bf16[768,768]{1,0:T(8,128)(2,1)} %all-gather.4.cloned.1.call-done) | copy-start | bytes 3538948
  351.6 315.9 %reduce-scatter.15.cloned.1.call-start = ((), (), s32[]{:S(2)}) async-start(), calls=%async_computation.10 | async-start | bytes 1327104 | tf_op jit(solution)/shard_map/reduce_scatter | solution.py:210
  361.0 308.5 %reduce-scatter.17.cloned.1.call-start = ((), (), s32[]{:S(2)}) async-start(), calls=%async_computation.11 | async-start | bytes 1327104 | tf_op jit(solution)/shard_map/reduce_scatter | solution.py:213
  380.8 293.9 %reduce-scatter.25.cloned.1.call-start = ((), (), s32[]{:S(2)}) async-start(), calls=%async_computation.15 | async-start | bytes 331776
  526.8 9.4 copy-start.3
  536.2 12.7 %copy-start.9 = (bf16[192,768]{0,1:T(8,128)(2,1)S(1)}, bf16[192,768]{0,1:T(8,128)(2,1)}, u32[]{:S(2)}) copy-start(bf16[192,768]{0,1:T(8,128)(2,1)} %copy-done.8) | copy-start | bytes 884740
  550.4 11.2 %copy-start.47 = (f32[3,64]{1,0:T(4,128)S(1)}, f32[3,64]{1,0:T(4,128)}, u32[]{:S(2)}) copy-start(f32[3,64]{1,0:T(4,128)} %add.204) | copy-start | bytes 2308
  588.0 11.4 %copy-start.5 = (bf16[3152,192]{0,1:T(8,128)(2,1)S(1)}, bf16[3152,192]{0,1:T(8,128)(2,1)}, u32[]{:S(2)}) copy-start(bf16[3152,192]{0,1:T(8,128)(2,1)} %copy-done.4) | copy-start | bytes 3631108
  589.2 15.2 %copy-start.45 = (f32[3,64]{1,0:T(4,128)S(1)}, f32[3,64]{1,0:T(4,128)}, u32[]{:S(2)}) copy-start(f32[3,64]{1,0:T(4,128)} %copy-done.44) | copy-start | bytes 2308
  604.3 71.8 %reduce-scatter.21.cloned.1.call-start = ((), (), s32[]{:S(2)}) async-start(), calls=%async_computation.13 | async-start | bytes 442368
  624.0 13.5 %copy-start.32 = (f32[3152]{0:T(1024)S(1)}, f32[3152]{0:T(1024)}, u32[]{:S(2)}) copy-start(f32[3152]{0:T(1024)} %copy-done.31) | copy-start | bytes 37828
  624.0 13.5 %copy-start.36 = (f32[3152]{0:T(1024)S(1)}, f32[3152]{0:T(1024)}, u32[]{:S(2)}) copy-start(f32[3152]{0:T(1024)} %copy-done.35) | copy-start | bytes 37828
  624.0 13.5 %copy-start.40 = (f32[768]{0:T(1024)S(1)}, f32[768]{0:T(1024)}, u32[]{:S(2)}) copy-start(f32[768]{0:T(1024)} %copy-done.39) | copy-start | bytes 9220
  624.0 13.4 %copy-start.53 = (f32[768]{0:T(1024)S(1)}, f32[768]{0:T(1024)}, u32[]{:S(2)}) copy-start(f32[768]{0:T(1024)} %copy-done.52) | copy-start | bytes 9220
  633.8 78.3 %reduce-scatter.19.cloned.1.call-start = ((), (), s32[]{:S(2)}) async-start(), calls=%async_computation.12 | async-start | bytes 1105920
  647.6 9.5 copy-start.19
  647.6 348.0 %all-reduce.10.cloned.1.call-start = ((), (), s32[]{:S(2)}) async-start(), calls=%async_computation.16 | async-start | bytes 19365888 | tf_op jit(solution)/shard_map/psum | solution.py:135
  647.9 9.2 copy-start.22
  663.0 12.5 %copy-start.49 = (f32[1,144]{1,0:T(1,128)S(1)}, f32[1,144]{1,0:T(1,128)}, u32[]{:S(2)}) copy-start(f32[1,144]{1,0:T(1,128)} %param.27) | copy-start | bytes 1732
  663.0 12.5 %copy-start.54 = (f32[1,144]{1,0:T(1,128)S(1)}, f32[1,144]{1,0:T(1,128)}, u32[]{:S(2)}) copy-start(f32[1,144]{1,0:T(1,128)} %param.39) | copy-start | bytes 1732
  663.0 12.5 %copy-start.55 = (f32[1,144]{1,0:T(1,128)S(1)}, f32[1,144]{1,0:T(1,128)}, u32[]{:S(2)}) copy-start(f32[1,144]{1,0:T(1,128)} %param.38) | copy-start | bytes 1732
  663.1 14.0 %copy-start.24 = (f32[192,96]{1,0:T(8,128)S(1)}, f32[192,96]{1,0:T(8,128)}, u32[]{:S(2)}) copy-start(f32[192,96]{1,0:T(8,128)} %param.23) | copy-start | bytes 221188
  663.1 14.0 %copy-start.37 = (f32[192,96]{1,0:T(8,128)S(1)}, f32[192,96]{1,0:T(8,128)}, u32[]{:S(2)}) copy-start(f32[192,96]{1,0:T(8,128)} %param.31) | copy-start | bytes 221188
  663.1 14.0 %copy-start.38 = (f32[192,96]{1,0:T(8,128)S(1)}, f32[192,96]{1,0:T(8,128)}, u32[]{:S(2)}) copy-start(f32[192,96]{1,0:T(8,128)} %param.30) | copy-start | bytes 221188
  663.1 376.8 %reduce-scatter.23.cloned.1.call-start = ((), (), s32[]{:S(2)}) async-start(), calls=%async_computation.14 | async-start | bytes 221184
  677.8 329.4 %copy-start.41 = (f32[768]{0:T(1024)S(1)}, f32[768]{0:T(1024)}, u32[]{:S(2)}) copy-start(f32[768]{0:T(1024)} %get-tuple-element.148) | copy-start | bytes 9220
  1007.3 33.5 %copy-start.43 = (f32[6,96]{1,0:T(8,128)S(1)}, f32[6,96]{1,0:T(8,128)}, u32[]{:S(2)}) copy-start(f32[6,96]{1,0:T(8,128)} %param.26) | copy-start | bytes 6916
  1007.3 33.5 %copy-start.50 = (f32[6,96]{1,0:T(8,128)S(1)}, f32[6,96]{1,0:T(8,128)}, u32[]{:S(2)}) copy-start(f32[6,96]{1,0:T(8,128)} %param.37) | copy-start | bytes 6916
  1007.3 33.5 %copy-start.51 = (f32[6,96]{1,0:T(8,128)S(1)}, f32[6,96]{1,0:T(8,128)}, u32[]{:S(2)}) copy-start(f32[6,96]{1,0:T(8,128)} %param.36) | copy-start | bytes 6916
  (24 other events, 112.5 us)
Sparse Core Ops, SparseCore 0:
  114.4 176.3 all-reduce.5
  351.7 175.0 all-reduce.7
  663.1 332.4 all-reduce.9
Sparse Core Ops, SparseCore 1:
  117.2 24.2 all-gather.3
  143.8 23.9 all-gather.5
  361.1 35.6 reduce-scatter.14
  400.4 36.6 reduce-scatter.16
  604.4 31.9 reduce-scatter.24
  639.4 33.8 reduce-scatter.20
  676.4 35.6 reduce-scatter.18
  1007.3 32.5 reduce-scatter.22
where the time goes:
time: 1060 us; the launch traced here: 1050 us
  waiting for transfers between devices  651 us (61%)
  matrix products  165 us (16%)
  other arithmetic  90.7 us (9%)
  local copies, waits for them, and re-layouts  77.5 us (7%)
  blocking collectives  46.1 us (4%)
  between operations  17.4 us (2%)
    psum x1, waiting for transfers between devices, per_device(): lax.psum(feed_terms.astype(jnp.bfloat16), 'tensor').astype(jnp.float32)  279 us
    psum x1, waiting for transfers between devices, per_device(): lax.psum(branch_terms.astype(jnp.bfloat16), 'tensor').astype(jnp.float32)  175 us
    psum x1, waiting for transfers between devices, per_device(): lax.psum(normed_two_terms.astype(jnp.bfloat16), 'tensor')  146 us
    unnamed x15, waiting for transfers between devices  51.2 us
    dot_general x3, matrix products, contract_cols(): lax.dot_general(left, right, (((1,), (1,)), ((), ())), preferred_element_...  36.4 us
    unnamed x144, local copies, waits for them, and re-layouts  26.2 us
    dot_general x3, matrix products, contract_rows(): lax.dot_general(left, right, (((0,), (0,)), ((), ())), preferred_element_...  23.2 us
  transfers between devices with their start and end apart: 11, of which 5 were waited for; matrix products, arithmetic and copies ran while one was open for 21% of the time, Pallas kernels for 0%

commit v1 on v0

v1 whole, which is shorter than its diff:
```python
import math
from functools import partial

import jax
import jax.numpy as jnp
from jax import lax
from jax.experimental import pallas as pl
from jax.experimental.pallas import tpu as pltpu
from jax.sharding import PartitionSpec as P

HEAD = 64
SEQ = 197
STEP = 10

EPS_NORM = 1e-06
EPS_ADAM = 1e-08
BETA_ONE = 0.9
BETA_TWO = 0.999
RATE_MATRIX = 0.05
RATE_VECTOR = 0.2
DECAY_MATRIX = 0.05

LOW = jnp.bfloat16
WIDE = jnp.float32
MESH = pl.DeviceIdType.MESH
ROWS = 16
BLOCK = 64
STRIP = 32
FAR_STEP = 64
FAR_SENT = 0
MEGA = 1024 * 1024
VMEM = pl.BlockSpec(memory_space=pltpu.VMEM)
ANY = pl.BlockSpec(memory_space=pl.ANY)


def round_up(value, unit):
    return -(-value // unit) * unit


def rem(left, right):
    return left % right if isinstance(left, int) else lax.rem(left, right)


def div(left, right):
    return left // right if isinstance(left, int) else lax.div(left, right)


def position():
    place, z = lax.axis_index("dp"), lax.axis_index("tensor")
    core, chip = rem(place, 2), div(place, 2)
    x, y = rem(chip, 2), div(chip, 2)
    return chip, core, z, y * 2 + (1 - x), (1 - y) * 2 + x, (1 - y) * 2 + (1 - x)


def z_partner(z, step):
    return z + rem(step, 2) * (1 - 2 * rem(z, 2)) + div(step, 2) * (2 - 4 * div(z, 2))


def chunk(n):
    late = div(n + 4, 8)
    return late * (1 + rem(n, 2)), (1 - late) * n + late * div(n - 4, 2)


def greet(wait=True):
    chip, core, z, x_chip, y_chip, _ = position()
    barrier = pltpu.get_barrier_semaphore()
    targets = [(x_chip * 2 + core, z), (y_chip * 2 + core, z), (chip * 2 + 1 - core, z)]
    targets += [(chip * 2 + core, z_partner(z, step)) for step in (1, 2, 3)]
    for target in targets:
        pl.semaphore_signal(barrier, inc=1, device_id=target, device_id_type=MESH)
    if wait:
        pl.semaphore_wait(barrier, len(targets))
    return barrier, len(targets)


def remote(src, dst, send, recv, target):
    return pltpu.make_async_remote_copy(
        src_ref=src, dst_ref=dst, send_sem=send, recv_sem=recv, device_id=target, device_id_type=MESH
    )


class Share:
    pieces = 2

    def __init__(self, part, whole, send, recv, own, far=range(pieces), far_size=None):
        self.far, self.far_size = far, far_size
        chip, core, self.z, _, _, _ = position()
        self.part, self.whole, self.send, self.recv = part, whole, send, recv
        self.here = chip * 2 + core
        self.size = part.shape[0] // self.pieces
        self.own = pltpu.make_async_copy(part, whole.at[self.z], own)
        self.inner = rem(self.z, 2) + div(self.z, 2) == 1

    def copy(self, kind, piece):
        z = self.z
        short = kind in (2, 4) and self.far_size
        rows = pl.ds(piece * self.size, self.far_size if short else self.size)
        block = z_partner(z, (0, 0, 1, 3, 2)[kind])
        src = (self.part if kind < 2 else self.whole.at[block]).at[rows]
        target = z_partner(z, (1, 3, 3, 1, 1)[kind])
        lane = (0, 1, 2, 1, 2)[kind]
        return remote(
            src, self.whole.at[block, rows], self.send.at[kind, piece], self.recv.at[lane, piece],
            (self.here, target),
        )

    def start(self):
        self.own.start()
        for piece in range(self.pieces):
            self.copy(0, piece).start()

        @pl.when(self.inner)
        def _():
            for piece in range(self.pieces):
                self.copy(1, piece).start()

    def pass_on(self, stage):
        near, piece = stage < self.pieces, stage % self.pieces

        @pl.when(self.inner)
        def _():
            if near:
                self.copy(0, piece).wait_recv()
                if piece in self.far:
                    self.copy(2, piece).start()
                self.copy(1, piece).wait_recv()
                self.copy(3, piece).start()
            elif piece in self.far:
                self.copy(2, piece).wait_recv()
                self.copy(4, piece).start()

    def finish(self):
        def each(kinds):
            for kind in kinds:
                for piece in self.far if kind in (2, 4) else range(self.pieces):
                    yield self.copy(kind, piece)

        @pl.when(jnp.logical_not(self.inner))
        def _():
            for copy in each((0, 3, 4)):
                copy.wait_recv()
            for copy in each((0,)):
                copy.wait_send()

        @pl.when(self.inner)
        def _():
            for copy in each(range(5)):
                copy.wait_send()

        self.own.wait()


def share_scratch():
    return [
        pltpu.SemaphoreType.DMA((5, Share.pieces)),
        pltpu.SemaphoreType.DMA((3, Share.pieces)),
        pltpu.SemaphoreType.DMA,
    ]


def dot(left, right, left_dim=1, right_dim=0):
    return lax.dot_general(
        left, right, (((left_dim,), (right_dim,)), ((), ())), preferred_element_type=WIDE
    )


def fill_unit(unit):
    row, column = (lax.broadcasted_iota(jnp.int32, unit.shape, dim) for dim in (0, 1))
    unit[...] = jnp.where(row == column, 1.0, 0.0).astype(LOW)


def flip(value, unit):
    count = value.shape[1]
    return dot(unit[:count, :count], value, 1, 1).astype(LOW)


def block_at(at):
    return pl.ds(pl.multiple_of(at * BLOCK, BLOCK), BLOCK)


def norm_parts(values):
    centre = values - jnp.mean(values, axis=-1, keepdims=True)
    factor = lax.rsqrt(jnp.mean(centre * centre, axis=-1, keepdims=True) + EPS_NORM)
    return centre * factor, factor


def norm_backward(grad_out, unit, factor, gain):
    scaled = grad_out * gain
    return factor * (
        scaled
        - jnp.mean(scaled, axis=-1, keepdims=True)
        - unit * jnp.mean(scaled * unit, axis=-1, keepdims=True)
    )


def fold(values):
    return jnp.sum(values.reshape(values.shape[0] // 8, 8, values.shape[1]), axis=0)


def attend(image, qkv, attended, mask, unit, turn, kept=None):
    padded, width = mask.shape[0], attended.shape[1]
    scale = 1.0 / math.sqrt(HEAD)
    spot = pl.ds(pl.multiple_of(image * padded, padded), padded)
    turn[0] = flip(qkv[spot, 2 * width : 3 * width], unit)
    for head in range(width // HEAD):
        lanes = head * HEAD
        query = qkv[spot, lanes : lanes + HEAD]
        key = qkv[spot, width + lanes : width + lanes + HEAD]
        scores = dot(key, query, 1, 1) + mask[...]
        highest = jnp.max(scores, axis=0, keepdims=True)
        exponent = jnp.exp((scores - highest) * scale)
        total = jnp.sum(exponent, axis=0, keepdims=True)
        prob = (exponent * (1.0 / total)).astype(LOW)
        if kept is not None:
            kept[image, head] = prob
        turn[1, lanes : lanes + HEAD, :] = dot(turn[0, lanes : lanes + HEAD, :], prob).astype(LOW)
    attended[spot, :] = flip(turn[1], unit)


def fill_mask(mask):
    mask[...] = jnp.where(lax.broadcasted_iota(jnp.int32, mask.shape, 0) < SEQ, 0.0, -1e30)


def gelu_parts(value):
    cdf = 0.5 * (1.0 + lax.erf(value * (1.0 / math.sqrt(2.0))))
    return cdf, jnp.exp(-0.5 * value * value) * (1.0 / math.sqrt(2.0 * math.pi))


class Rows:
    def __init__(self, src, window, sems, begin, images, padded):
        self.src, self.window, self.sems = src, window, sems
        self.begin, self.images, self.padded = begin, images, padded

    def copy(self, image):
        begin = (self.begin + image) * SEQ
        last = self.src.shape[0] - SEQ
        aligned = div(begin, ROWS) * ROWS - ROWS * div(begin, last)
        rows = pl.ds(pl.multiple_of(aligned, ROWS), self.window.shape[1])
        copy = pltpu.make_async_copy(self.src.at[rows], self.window.at[image], self.sems.at[image])
        return copy, begin - aligned

    def fetch(self):
        for image in range(self.images):
            self.copy(image)[0].start()

    def place(self, dst):
        span, padded = self.window.shape[1], self.padded

        @pl.loop(0, self.images)
        def _(image):
            copy, shift = self.copy(image)
            copy.wait()
            moved = pltpu.roll(self.window[image].astype(WIDE), rem(span - shift, span), axis=0)[:padded]
            inside = lax.broadcasted_iota(jnp.int32, (padded, 1), 0) < SEQ
            spot = pl.ds(pl.multiple_of(image * padded, padded), padded)
            dst[spot, :] = jnp.where(inside, moved, 0.0).astype(LOW)


def far_block(z, tensors):
    return (tensors - 1) * (1 - div(z, tensors // 2))


def pack_images(values, work, images, padded):
    for image in range(images):
        work[image * SEQ : (image + 1) * SEQ, :] = values[image * padded : image * padded + SEQ, :]


def arrange(raw, shard, vec, slab, width):
    qkv, out, up, down_t, shared, split = raw
    for at in range(3):
        shard[0, :, at * width : (at + 1) * width] = qkv[at].astype(LOW)
    shard[0, :, 3 * width :] = out[...].T.astype(LOW)
    shard[1] = up[...].astype(LOW)
    shard[2] = down_t[...].astype(LOW)
    vec[...] = jnp.zeros_like(vec)
    vec[:6, :slab] = shared[...]
    count = split.shape[1]
    groups = count // 6
    column = jnp.broadcast_to(split[...], (8, count)).T[:, :1]
    row, lane = (lax.broadcasted_iota(jnp.int32, (count, 128), dim) for dim in (0, 1))
    attention = jnp.where(lane < groups, 6 * lane, jnp.where(lane < 2 * groups, 6 * (lane - groups) + 1, -1))
    hidden = jnp.where(lane < 4 * groups, 6 * div(lane, 4) + 2 + rem(lane, 4), -1)
    for at, wanted in ((6, attention), (7, hidden)):
        vec[at : at + 1, :] = jnp.sum(jnp.where(row == wanted, column, 0.0), axis=0, keepdims=True)


def forward_kernel(
    tokens, cotangent, *refs, linked,
):
    count = 6 if linked else 2
    forward_body(tokens, cotangent, refs[:count], *refs[count:], linked=linked)


def forward_body(
    tokens, cotangent, sources,
    packed, weights_out, own_out, back_out, back_t_out, gains_out, biases_out,
    normed_out, qkv_out, probs_out, attended_out, middle_out, two_out, hidden_out, slope_out,
    held, vec_held, gains, biases, window, own, back, back_t,
    normed, qkv, probs, attended, middle, two, hidden, slope, work, feed,
    mask, unit, turn, in_sem, row_sem, out_sem, act_sem, weight_sem, vec_send, vec_recv, send, recv, *own_parts,
    linked,
):
    tensors = held.shape[1]
    model, hidden_width = own.shape[1], held.shape[-1]
    width = hidden_width // 4
    heads = width // HEAD
    images, padded = probs.shape[1], probs.shape[-1]
    rows = images * padded
    scale = 1.0 / math.sqrt(HEAD)
    chunks = 3 * tensors
    z = lax.axis_index("tensor")

    own_tokens = Rows(tokens, window, row_sem, z * images, images, padded)
    own_cotangent = Rows(cotangent, window, row_sem, z * images, images, padded)

    def fill_constants():
        fill_unit(unit)
        fill_mask(mask)
        biases[...] = jnp.zeros_like(biases)

    own_tokens.fetch()

    if linked:
        chip, core, _, x_chip, y_chip, far_chip = position()
        x_dev, y_dev, other = (x_chip * 2 + core, z), (y_chip * 2 + core, z), (chip * 2 + 1 - core, z)
        half = held.shape[4] // 2
        weights, vec, *raw = own_parts
        raw_copies = [
            pltpu.make_async_copy(src, dst, vec_send.at[div(at, 3), rem(at, 3)])
            for at, (src, dst) in enumerate(zip(sources, raw))
        ]
        for copy in raw_copies:
            copy.start()
        barrier = greet(wait=False)
        for copy in raw_copies:
            copy.wait()
        arrange(raw, weights, vec, held.shape[4], width)
        pl.semaphore_wait(*barrier)

        def link(n, kind):
            group, step = chunk(n)
            t = z_partner(z, step)
            sems = (send.at[n, kind], recv.at[n, kind])
            spot = held.at[group, t, chip, core]
            if kind == 0:
                to = (chip * 2 + core, t)
                return remote(weights.at[group], held.at[group, z, chip, core], *sems, to)
            if kind == 1:
                return remote(spot, spot, *sems, x_dev)
            if kind == 2:
                return remote(spot, spot, *sems, y_dev)
            if kind == 3:
                spot = held.at[group, t, x_chip, core, pl.ds(0, half)]
                return remote(spot, spot, *sems, y_dev)
            if kind == 4:
                spot = held.at[group, t, y_chip, core, pl.ds(half, half)]
                return remote(spot, spot, *sems, x_dev)
            spot = held.at[group, t, :, core]
            return remote(spot, spot, *sems, other)

        def vec_link(step, kind):
            t = z_partner(z, step)
            sems = (vec_send.at[step, kind], vec_recv.at[step, kind])
            if kind == 0:
                return remote(vec, vec_held.at[z, chip, core], *sems, (chip * 2 + core, t))
            spot = vec_held.at[t, x_chip if kind == 3 else chip, core]
            if kind == 5:
                spot = vec_held.at[t, :, core]
            return remote(spot, spot, *sems, {1: x_dev, 2: y_dev, 3: y_dev, 5: other}[kind])

        own_copies = [
            pltpu.make_async_copy(weights.at[group], held.at[group, z, chip, core], in_sem.at[group, 0])
            for group in range(3)
        ] + [pltpu.make_async_copy(vec, vec_held.at[z, chip, core], in_sem.at[3, 0])]
        for copy in own_copies:
            copy.start()
        for step in (1, 2, 3):
            vec_link(step, 0).start()
        for n in range(chunks):
            if chunk(n)[1]:
                link(n, 0).start()

        def first(n):
            if isinstance(n, int):
                if chunk(n)[1]:
                    link(n, 0).wait_recv()
            else:

                @pl.when(chunk(n)[1] > 0)
                def _():
                    link(n, 0).wait_recv()

            link(n, 1).start()
            link(n, 2).start()

        def second(n):
            link(n, 1).wait_recv()
            link(n, 3).start()
            link(n, 2).wait_recv()
            link(n, 4).start()

        def third(n):
            link(n, 3).wait_recv()
            link(n, 4).wait_recv()
            link(n, 5).start()

        def arrived(n):
            link(n, 5).wait_recv()

        def serve(n):
            first(n + 2)
            second(n)
            third(n - 2)

        for copy in own_copies:
            copy.wait()
        first(0)
        for step in range(4):
            if step:
                vec_link(step, 0).wait_recv()
            vec_link(step, 1).start()
            vec_link(step, 2).start()
        own_tokens.place(own)
        own_cotangent.fetch()
        first(1)
        for step in range(4):
            vec_link(step, 1).wait_recv()
            vec_link(step, 3).start()
        second(0)
        fill_constants()
        for step in range(4):
            vec_link(step, 2).wait_recv()
            vec_link(step, 3).wait_recv()
            vec_link(step, 5).start()
        third(0)
        first(2)
        own_cotangent.place(back)
        back_t[...] = back[...].T
        second(1)
        first(3)
        for step in range(4):
            vec_link(step, 5).wait_recv()
    else:
        weights, vec = sources

        def local(n):
            group, step = chunk(n)
            return pltpu.make_async_copy(
                weights.at[group, step], held.at[group, step, 0, 0], in_sem.at[group, step]
            )

        for n in range(chunks):
            local(n).start()
        copy = pltpu.make_async_copy(vec, vec_held, in_sem.at[3, 0])
        copy.start()
        copy.wait()

        def arrived(n):
            local(n).wait()

        own_tokens.place(own)
        own_cotangent.fetch()
        fill_constants()
        own_cotangent.place(back)
        back_t[...] = back[...].T

    def tensor_at(step):
        return z_partner(z, step) if linked else step

    def keep_weights(n):
        group, step = chunk(n)
        t = tensor_at(step)
        return pltpu.make_async_copy(held.at[group, t], weights_out.at[group, t], weight_sem.at[n])

    def ready(n):
        arrived(n)
        if linked:
            keep_weights(n).start()

    def save(at, src, dst):
        return pltpu.make_async_copy(src, dst, out_sem.at[at])

    places = vec_held.shape[1] * vec_held.shape[2]
    slab, share = model // places, width // places

    @pl.loop(0, tensors)
    def _(t):
        for place in range(places):
            piece = vec_held[t, place // 2, place % 2]
            gains[t, :, place * slab : (place + 1) * slab] = piece[:, :slab]
            biases[t, :, place * share : (place + 1) * share] = piece[:, :share]
            begin = 2 * width + place * share
            biases[t, :, begin : begin + share] = piece[:, share : 2 * share]

    saves = [save(8, own, own_out), save(9, gains, gains_out), save(10, back, back_out)]
    saves += [save(11, biases, biases_out), save(12, back_t, back_t_out)]
    for copy in saves:
        copy.start()

    @pl.loop(0, rows // BLOCK)
    def _(at):
        block = block_at(at)
        inputs = own[block, :].astype(WIDE)
        unit, _ = norm_parts(inputs)
        normed[block, :] = (unit * gains[0, 0:1, :] + gains[0, 1:2, :]).astype(LOW)
        middle[block, :] = inputs + gains[0, 4:5, :]

    saves.append(save(0, normed, normed_out))
    saves[-1].start()

    @pl.loop(0, tensors)
    def _(step):
        t = tensor_at(step)
        ready(step)
        wide = held[0, t, :, :, :, : 3 * width].reshape(model, 3 * width)
        qkv[t] = (dot(normed[...], wide) + biases[t, 6:7, :]).astype(LOW)

        @pl.loop(0, 2)
        def _(part):
            for at in range(images // 2):
                image = part * (images // 2) + at
                attend(image, qkv.at[t], attended.at[t], mask, unit, turn.at[at], probs.at[t])

            if linked:

                @pl.when(jnp.logical_and(part == 0, step == 0))
                def _():
                    first(4)
                    second(2)

                @pl.when(jnp.logical_and(part == 0, step == 1))
                def _():
                    serve(4)

                @pl.when(part == 1)
                def _():
                    serve(3 + step + div(step + 3, 4))

        out = held[0, t, :, :, :, 3 * width :].reshape(model, width)
        middle[...] += dot(attended[t], out, 1, 1)

    saves += [
        save(1, qkv, qkv_out),
        save(2, probs, probs_out),
        save(3, attended, attended_out),
        save(4, middle, middle_out),
    ]
    for copy in saves[-4:]:
        copy.start()

    @pl.loop(0, rows // BLOCK)
    def _(at):
        block = block_at(at)
        values = middle[block, :]
        unit, _ = norm_parts(values)
        two[block, :] = (unit * gains[0, 2:3, :] + gains[0, 3:4, :]).astype(LOW)
        feed[block, :] = values + gains[0, 5:6, :]

    saves.append(save(5, two, two_out))
    saves[-1].start()

    half_rows, wide_lanes = rows // 2, 256
    halves = [pl.ds(0, half_rows), pl.ds(half_rows, half_rows)]

    def keep_acts(step):
        t = tensor_at(step)
        return [
            pltpu.make_async_copy(src.at[t], dst.at[t], act_sem.at[at, step])
            for at, (src, dst) in enumerate(((hidden, hidden_out), (slope, slope_out)))
        ]

    def up_part(half, step, lanes):
        weight = held[1, tensor_at(step), :, :, :, lanes].reshape(model, wide_lanes)
        work[halves[half], lanes] = dot(two[halves[half], :], weight)

    def act_part(half, step, at):
        t = tensor_at(step)
        block = pl.ds(half * half_rows + at * STRIP, STRIP)
        value = work[block, :] + gains[t, 7:8, :]
        cdf, density = gelu_parts(value)
        hidden[t, block, :] = (value * cdf).astype(LOW)
        slope[t, block, :] = (cdf + value * density).astype(LOW)

    def down_part(half, step, lanes):
        t = tensor_at(step)
        weight = held[2, t].reshape(model, hidden_width)[lanes]
        feed[halves[half], lanes] += dot(hidden[t, halves[half], :], weight, 1, 1)

    def together(up=None, act=None, down=None):
        lanes = [slice(at, at + wide_lanes) for at in range(0, hidden_width, wide_lanes)]
        products = [partial(up_part, *up, lane) for lane in lanes] if up else []
        products += [partial(down_part, *down, lane) for lane in lanes] if down else []
        acts = [partial(act_part, *act, at) for at in range(half_rows // STRIP)] if act else []
        every = -(-len(acts) // max(len(products), 1))
        for at, product in enumerate(products):
            product()
            for part in acts[at * every : (at + 1) * every]:
                part()
        for part in acts[len(products) * every :]:
            part()

    ready(tensors)
    together(up=(0, 0))
    if linked:
        serve(8)
    together(up=(1, 0), act=(0, 0))
    if linked:
        serve(9)

    @pl.loop(1, tensors)
    def _(step):
        ready(2 * step + 3)
        ready(2 * step + 4)
        together(up=(0, step), act=(1, step - 1), down=(0, step - 1))
        for copy in keep_acts(step - 1):
            copy.start()
        if linked:

            @pl.when(step == 1)
            def _():
                second(10)
                third(8)

            @pl.when(step == 2)
            def _():
                third(10)

        together(up=(1, step), act=(0, step), down=(1, step - 1))
        if linked:

            @pl.when(step == 1)
            def _():
                second(11)
                third(9)

            @pl.when(step == 2)
            def _():
                third(11)

    last = tensors - 1
    ready(chunks - 1)
    together(act=(1, last), down=(0, last))
    for copy in keep_acts(last):
        copy.start()
    together(down=(1, last))
    for step in range(tensors):
        saves += keep_acts(step)
    pack_images(feed, work, images, padded)
    packed[...] = work[: packed.shape[0], :].astype(LOW)
    for copy in saves:
        copy.wait()
    if linked:
        for step in range(4):
            for kind in (0, 1, 2, 3, 5):
                if kind or step:
                    vec_link(step, kind).wait_send()

        @pl.loop(0, chunks)
        def _(n):
            @pl.when(chunk(n)[1] > 0)
            def _():
                link(n, 0).wait_send()

            for kind in range(1, 6):
                link(n, kind).wait_send()
            keep_weights(n).wait()


def forward(tokens, cotangent, sources, images, width, tensors, places, linked):
    model, hidden_width = tokens.shape[1], 4 * width
    padded, heads = round_up(SEQ, ROWS), width // HEAD
    rows, packed_rows = images * padded, round_up(images * SEQ, 2 * ROWS)
    if linked:
        blocks = (3, tensors, places // 2, 2, model // places, hidden_width)
    else:
        blocks = (3, tensors, 1, 1, model, hidden_width)
    kept = (
        ((rows, model), LOW),
        ((tensors, rows, 3 * width), LOW),
        ((tensors, images, heads, padded, padded), LOW),
        ((tensors, rows, width), LOW),
        ((rows, model), WIDE),
        ((rows, model), LOW),
        ((tensors, rows, hidden_width), LOW),
        ((tensors, rows, hidden_width), LOW),
    )
    outs = (
        ((packed_rows, model), LOW),
        (blocks if linked else (8, 128), LOW),
        ((rows, model), LOW),
        ((rows, model), LOW),
        ((model, rows), LOW),
        ((tensors, 8, model), WIDE),
        ((tensors, 8, 3 * width), WIDE),
    ) + kept
    dma = pltpu.SemaphoreType.DMA
    own_parts = []
    if linked:
        own_parts = [pltpu.VMEM((3, model // places, hidden_width), LOW), pltpu.VMEM((8, 128), WIDE)]
        own_parts += [pltpu.VMEM(source.shape, WIDE) for source in sources]
    return pl.pallas_call(
        partial(forward_kernel, linked=linked),
        out_shape=[jax.ShapeDtypeStruct(shape, dtype) for shape, dtype in outs],
        in_specs=[ANY] * (2 + len(sources)),
        out_specs=[VMEM] + [ANY] * (len(outs) - 1),
        scratch_shapes=[
            pltpu.VMEM(blocks, LOW),
            pltpu.VMEM((tensors, places // 2, 2, 8, 128), WIDE),
            pltpu.VMEM((tensors, 8, model), WIDE),
            pltpu.VMEM((tensors, 8, 3 * width), WIDE),
            pltpu.VMEM((images, padded + ROWS, model), LOW),
            pltpu.VMEM((rows, model), LOW),
            pltpu.VMEM((rows, model), LOW),
            pltpu.VMEM((model, rows), LOW),
        ]
        + [pltpu.VMEM(shape, dtype) for shape, dtype in kept]
        + [
            pltpu.VMEM((rows, hidden_width), WIDE),
            pltpu.VMEM((rows, model), WIDE),
            pltpu.VMEM((padded, padded), WIDE),
            pltpu.VMEM((padded, padded), LOW),
            pltpu.VMEM((images // 2, 2, width, padded), LOW),
            dma((4, tensors)),
            dma((images,)),
            dma((13,)),
            dma((2, tensors)),
            dma((3 * tensors,)),
            dma((4, 6)),
            dma((4, 6)),
            dma((3 * tensors, 6)),
            dma((3 * tensors, 6)),
        ]
        + own_parts,
        compiler_params=pltpu.CompilerParams(
            vmem_limit_bytes=58 * MEGA, has_side_effects=True, **({"collective_id": 0} if linked else {})
        ),
        name="forward",
    )(tokens, cotangent, *sources)


def chain_kernel(
    packed, tokens_in, cotangent, cot_t_in, gains, weights, qkv_in, probs_in, middle_in, slope_in, hidden_in,
    packed_grad, block_out, hidden_back_out, back_low_out, qkv_back_out, vec_grads, down_grads,
    tokens, cot_t, mixed, stream, slopes, acts, staged, qkv, probs, middle, work, total, back, back_low, hidden_back, attended_back,
    qkv_back, rows_eight, bias_rows, unit, turn, in_sem, stream_sem, out_sem, down_sem, *share_sems,
    linked,
):
    rows, model = cotangent.shape
    tensors, hidden_width = weights.shape[1], weights.shape[-1]
    width = hidden_width // 4
    heads = width // HEAD
    images, padded = probs.shape[1], probs.shape[-1]
    scale = 1.0 / math.sqrt(HEAD)
    places = vec_grads.shape[1]
    slab, part = model // places, width // places

    if linked:
        greet()
        shared = Share(packed, block_out, *share_sems, far=())
        shared.start()

    def fetch(t):
        slot = rem(t, 2)
        pairs = (
            (weights.at[2, t], stream.at[slot, 0]),
            (slope_in.at[t], slopes.at[slot]),
            (weights.at[1, t], stream.at[slot, 1]),
            (hidden_in.at[t], acts.at[slot]),
        )
        return [
            pltpu.make_async_copy(src, dst, stream_sem.at[slot, at]) for at, (src, dst) in enumerate(pairs)
        ]

    for copy in fetch(0):
        copy.start()
    turned = pltpu.make_async_copy(cot_t_in, cot_t, in_sem.at[5])
    turned.start()
    pairs = (
        (middle_in, middle), (weights.at[0], mixed), (qkv_in, qkv), (probs_in, probs), (tokens_in, tokens),
    )
    loads = [pltpu.make_async_copy(src, dst, in_sem.at[at]) for at, (src, dst) in enumerate(pairs)]
    for copy in loads:
        copy.start()
    total[...] = jnp.zeros_like(total)
    rows_eight[...] = jnp.zeros_like(rows_eight)
    fill_unit(unit)

    def keep_down(t):
        slot = rem(t, 2)
        return pltpu.make_async_copy(staged.at[slot], down_grads.at[t], down_sem.at[slot])

    def keep_hidden(t):
        slot = rem(t, 2)
        return pltpu.make_async_copy(hidden_back.at[slot], hidden_back_out.at[t], out_sem.at[slot])

    @pl.loop(0, tensors)
    def _(t):
        slot = rem(t, 2)

        @pl.when(t + 1 < tensors)
        def _():
            for copy in fetch(t + 1):
                copy.start()

        @pl.when(t > 1)
        def _():
            keep_hidden(t - 2).wait()
            keep_down(t - 2).wait()

        copies = fetch(t)
        copies[0].wait()
        work[...] = dot(cotangent[...], stream[slot, 0].reshape(model, hidden_width))
        copies[1].wait()

        def through(at, sums):
            block = block_at(at)
            low = (work[block, :] * slopes[slot, block, :].astype(WIDE)).astype(LOW)
            hidden_back[slot, block, :] = low
            return sums + fold(low.astype(WIDE))

        sums = lax.fori_loop(0, rows // BLOCK, through, jnp.zeros((8, hidden_width), WIDE))
        rows_eight[t, 7:8, :] = jnp.sum(sums, axis=0, keepdims=True)
        keep_hidden(t).start()
        copies[2].wait()
        total[...] += dot(hidden_back[slot], stream[slot, 1].reshape(model, hidden_width), 1, 1)
        copies[3].wait()

        @pl.when(t == 0)
        def _():
            turned.wait()

        staged[slot] = dot(cot_t[...], acts[slot]).astype(LOW).reshape(staged.shape[1:])
        keep_down(t).start()
        if linked:

            @pl.when(t == tensors // 2)
            def _():
                shared.pass_on(0)
    loads[0].wait()

    def second_norm(at, sums):
        block = block_at(at)
        unit, factor = norm_parts(middle[block, :])
        grad_out = total[block, :]
        from_above = cotangent[block, :].astype(WIDE)
        value = from_above + norm_backward(grad_out, unit, factor, gains[0, 2:3, :])
        back[block, :] = value
        back_low[block, :] = value.astype(LOW)
        parts = (grad_out * unit, grad_out, value, from_above)
        return tuple(old + fold(part) for old, part in zip(sums, parts))

    zero = jnp.zeros((8, model), WIDE)
    sums = lax.fori_loop(0, rows // BLOCK, second_norm, (zero,) * 4)

    def shared_sum(row, value):
        row_sum = jnp.sum(value, axis=0, keepdims=True)
        for t in range(tensors):
            rows_eight[t, row : row + 1, :] = row_sum

    for at, value in enumerate(sums):
        shared_sum(at + 2, value)
    keep_back = pltpu.make_async_copy(back_low, back_low_out, out_sem.at[2])
    keep_back.start()
    if linked:
        shared.pass_on(1)
    for copy in loads[1:]:
        copy.wait()
    total[...] = jnp.zeros_like(total)
    for slot in range(2):
        keep_hidden(slot).wait()
        keep_down(slot).wait()

    def keep_qkv(t):
        slot = rem(t, 2)
        return pltpu.make_async_copy(qkv_back.at[slot], qkv_back_out.at[t], out_sem.at[slot])

    @pl.loop(0, tensors)
    def _(t):
        slot = rem(t, 2)

        @pl.when(t > 1)
        def _():
            keep_qkv(t - 2).wait()

        out = mixed[t, :, :, :, 3 * width :].reshape(model, width)
        attended_back[...] = dot(back_low[...], out).astype(LOW)

        def attend_back(image, turn):
            spot = pl.ds(pl.multiple_of(image * padded, padded), padded)
            turn[0] = flip(qkv[t, spot, width : 2 * width], unit)
            for head in range(heads):
                lanes = head * HEAD
                query = qkv[t, spot, lanes : lanes + HEAD]
                value = qkv[t, spot, 2 * width + lanes : 2 * width + lanes + HEAD]
                grad = attended_back[spot, lanes : lanes + HEAD]
                prob_low = probs[t, image, head]
                prob = prob_low.astype(WIDE)
                weighted = prob * dot(value, grad, 1, 1)
                score_back = weighted - prob * jnp.sum(weighted, axis=0, keepdims=True)
                score_back = (score_back * scale).astype(LOW)
                query_back = dot(turn[0, lanes : lanes + HEAD, :], score_back)
                turn[1, lanes : lanes + HEAD, :] = query_back.astype(LOW)
                begin = width + lanes
                qkv_back[slot, spot, begin : begin + HEAD] = dot(score_back, query).astype(LOW)
                begin = 2 * width + lanes
                qkv_back[slot, spot, begin : begin + HEAD] = dot(prob_low, grad).astype(LOW)

            qkv_back[slot, spot, :width] = flip(turn[1], unit)

        @pl.loop(0, images // 2)
        def _(pair):
            for at in range(2):
                attend_back(2 * pair + at, turn.at[at])

        keep_qkv(t).start()
        bias_rows[t] = jnp.sum(qkv_back[slot].astype(WIDE), axis=0, keepdims=True)
        wide = mixed[t, :, :, :, : 3 * width].reshape(model, 3 * width)
        total[...] += dot(qkv_back[slot], wide, 1, 1)
    def first_norm(at, sums):
        block = block_at(at)
        unit, factor = norm_parts(tokens[block, :].astype(WIDE))
        grad_out = total[block, :]
        back[block, :] += norm_backward(grad_out, unit, factor, gains[0, 0:1, :])
        parts = (grad_out * unit, grad_out)
        return tuple(old + fold(part) for old, part in zip(sums, parts))

    sums = lax.fori_loop(0, rows // BLOCK, first_norm, (zero,) * 2)
    for at, value in enumerate(sums):
        shared_sum(at, value)
    pack_images(back, work, images, padded)
    packed_grad[...] = work[: packed_grad.shape[0], :].astype(LOW)

    vec_grads[...] = jnp.zeros_like(vec_grads)

    @pl.loop(0, tensors)
    def _(t):
        for place in range(places):
            vec_grads[t, place, :, :slab] = rows_eight[t, :, place * slab : (place + 1) * slab]
            vec_grads[t, place, 6:7, :part] = bias_rows[t, :, place * part : (place + 1) * part]
            begin = 2 * width + place * part
            vec_grads[t, place, 6:7, part : 2 * part] = bias_rows[t, :, begin : begin + part]

    keep_back.wait()
    for slot in range(2):
        keep_qkv(slot).wait()
    if linked:
        shared.finish()


def chain(packed, tokens, cotangent, cot_t, gains, weights, qkv, probs, middle, slope, hidden, places, linked):
    rows, model = tokens.shape
    tensors, hidden_width = weights.shape[1], weights.shape[-1]
    width = hidden_width // 4
    dma = pltpu.SemaphoreType.DMA
    whole = (tensors,) + packed.shape if linked else (8, 128)
    outs = (
        (packed.shape, LOW),
        (whole, LOW),
        ((tensors, rows, hidden_width), LOW),
        ((rows, model), LOW),
        ((tensors, rows, 3 * width), LOW),
        ((tensors, places, 8, 128), WIDE),
        (weights.shape[1:], LOW),
    )
    return pl.pallas_call(
        partial(chain_kernel, linked=linked),
        out_shape=[jax.ShapeDtypeStruct(shape, dtype) for shape, dtype in outs],
        in_specs=[ANY, ANY, VMEM, ANY, VMEM] + [ANY] * 6,
        out_specs=[VMEM] + [ANY] * 4 + [VMEM, ANY],
        scratch_shapes=[
            pltpu.VMEM((rows, model), LOW),
            pltpu.VMEM((model, rows), LOW),
            pltpu.VMEM(weights.shape[1:], LOW),
            pltpu.VMEM((2, 2) + weights.shape[2:], LOW),
            pltpu.VMEM((2, rows, hidden_width), LOW),
            pltpu.VMEM((2, rows, hidden_width), LOW),
            pltpu.VMEM((2,) + weights.shape[2:], LOW),
            pltpu.VMEM(qkv.shape, LOW),
            pltpu.VMEM(probs.shape, LOW),
            pltpu.VMEM((rows, model), WIDE),
            pltpu.VMEM((rows, hidden_width), WIDE),
            pltpu.VMEM((rows, model), WIDE),
            pltpu.VMEM((rows, model), WIDE),
            pltpu.VMEM((rows, model), LOW),
            pltpu.VMEM((2, rows, hidden_width), LOW),
            pltpu.VMEM((rows, width), LOW),
            pltpu.VMEM((2, rows, 3 * width), LOW),
            pltpu.VMEM((tensors, 8, model), WIDE),
            pltpu.VMEM((tensors, 1, 3 * width), WIDE),
            pltpu.VMEM(probs.shape[-2:], LOW),
            pltpu.VMEM((2, 2, width, probs.shape[-1]), LOW),
            dma((6,)),
            dma((2, 4)),
            dma((3,)),
            dma((2,)),
        ]
        + (share_scratch() if linked else []),
        compiler_params=pltpu.CompilerParams(
            vmem_limit_bytes=58 * MEGA, has_side_effects=True, **({"collective_id": 1} if linked else {})
        ),
        name="chain",
    )(packed, tokens, cotangent, cot_t, gains, weights, qkv, probs, middle, slope, hidden)


class Far:
    def __init__(
        self, tokens, weights, gains, biases, out,
        held, window, inputs, normed, qkv, attended, middle, two, work, hidden, packed, mask, unit, turn,
        weight_sem, row_sem, out_sem,
    ):
        self.weights, self.gains, self.biases = weights, gains, biases
        self.held, self.weight_sem = held, weight_sem
        self.inputs, self.normed, self.qkv, self.attended = inputs, normed, qkv, attended
        self.middle, self.two, self.work, self.hidden = middle, two, work, hidden
        self.packed, self.mask, self.unit, self.turn = packed, mask, unit, turn
        self.tensors = weights.shape[1]
        self.rows, self.model = inputs.shape
        self.hidden_width = weights.shape[-1]
        self.width = self.hidden_width // 4
        self.padded = mask.shape[0]
        self.images = self.rows // self.padded
        block = far_block(lax.axis_index("tensor"), self.tensors)
        first = block * (self.images + FAR_SENT) + FAR_SENT
        self.source = Rows(tokens, window, row_sem, first, self.images, self.padded)
        self.store = pltpu.make_async_copy(packed, out, out_sem)

    def weight(self, at):
        group, t = chunk(at)
        slot = rem(at, 2)
        return pltpu.make_async_copy(self.weights.at[group, t], self.held.at[slot], self.weight_sem.at[slot])

    def start(self):
        self.source.fetch()
        self.weight(0).start()
        self.weight(1).start()

    def each_block(self, body):
        @pl.loop(0, self.rows // FAR_STEP)
        def _(at):
            body(pl.ds(pl.multiple_of(at * FAR_STEP, FAR_STEP), FAR_STEP))

    def first_norm(self):
        fill_unit(self.unit)
        fill_mask(self.mask)
        self.source.place(self.inputs)

        def body(block):
            inputs = self.inputs[block, :].astype(WIDE)
            unit, _ = norm_parts(inputs)
            self.normed[block, :] = (unit * self.gains[0, 0:1, :] + self.gains[0, 1:2, :]).astype(LOW)
            self.middle[block, :] = inputs + self.gains[0, 4:5, :]

        self.each_block(body)

    def attention(self, t):
        width = self.width
        slot = rem(t, 2)
        self.weight(t).wait()
        weight = self.held[slot, :, :, :, : 3 * width].reshape(self.model, 3 * width)
        self.qkv[...] = (dot(self.normed[...], weight) + self.biases[t, 6:7, :]).astype(LOW)

        @pl.loop(0, self.images // 2)
        def _(pair):
            for at in range(2):
                attend(2 * pair + at, self.qkv, self.attended, self.mask, self.unit, self.turn.at[at])

        weight = self.held[slot, :, :, :, 3 * width :].reshape(self.model, width)
        self.middle[...] += dot(self.attended[...], weight, 1, 1)
        self.weight(t + 2).start()

    def second_norm(self):
        def body(block):
            values = self.middle[block, :]
            unit, _ = norm_parts(values)
            self.two[block, :] = (unit * self.gains[0, 2:3, :] + self.gains[0, 3:4, :]).astype(LOW)
            self.middle[block, :] = values + self.gains[0, 5:6, :]

        self.each_block(body)

    def up(self, t):
        at = self.tensors + 2 * t
        self.weight(at).wait()
        self.work[...] = dot(self.two[...], self.held[rem(at, 2)].reshape(self.model, self.hidden_width))

        @pl.when(t + 1 < self.tensors)
        def _():
            self.weight(at + 2).start()

        def body(block):
            value = self.work[block, :] + self.gains[t, 7:8, :]
            self.hidden[block, :] = (value * gelu_parts(value)[0]).astype(LOW)

        self.each_block(body)

    def down(self, t):
        at = self.tensors + 2 * t + 1
        self.weight(at).wait()
        weight = self.held[rem(at, 2)].reshape(self.model, self.hidden_width)
        self.middle[...] += dot(self.hidden[...], weight, 1, 1)

        @pl.when(t + 1 < self.tensors)
        def _():
            self.weight(at + 2).start()

    def step(self, n):
        tensors = self.tensors

        @pl.when(n == 0)
        def _():
            self.first_norm()

        @pl.when(jnp.logical_and(n > 0, n <= tensors))
        def _():
            self.attention(n - 1)

        @pl.when(n == tensors + 1)
        def _():
            self.second_norm()

        @pl.when(jnp.logical_and(n > tensors + 1, n <= 2 * tensors + 1))
        def _():
            self.up(n - tensors - 2)
            self.down(n - tensors - 2)

        @pl.when(n == 2 * tensors + 2)
        def _():
            self.finish()

    def finish(self):
        pack_images(self.middle, self.work, self.images, self.padded)
        self.packed[...] = self.work[: self.packed.shape[0], :].astype(LOW)
        self.store.start()

    def wait(self):
        self.store.wait()


def grads_kernel(
    packed, vec_grads, normed_in, two_in, back_in, qkv_back_in, attended_in, hidden_back_in, down_grads,
    tokens, weights, gains, biases,
    tokens_grad, total_out, vec_out, far_out,
    flat, normed_t, two_t, back_t, acts, mixed_acts, attended_acts, staged,
    pair, x_half, y_half, x_full, y_full, z_sum, vec_pair, vec_x, vec_y, vec_z,
    in_sem, act_sem, keep_sem, vec_send, vec_recv, send, recv, *more,
    linked,
):
    share_sems, far_scratch = more[:3], more[3:]
    tensors, rows, hidden_width = hidden_back_in.shape
    width = hidden_width // 4
    chunks = 3 * tensors
    z = lax.axis_index("tensor")

    def tensor_at(step):
        return z_partner(z, tensors - 1 - step) if linked else step

    def fetch(n, group):
        t, slot = tensor_at(chunk(n)[1]), rem(n, 2)
        pairs = (
            [(qkv_back_in, mixed_acts), (attended_in, attended_acts)],
            [(hidden_back_in, acts)],
            [(down_grads, staged)],
        )[group]
        return [
            pltpu.make_async_copy(src.at[t], dst.at[rem(n, dst.shape[0])], act_sem.at[slot, at])
            for at, (src, dst) in enumerate(pairs)
        ]

    def start(copies):
        for copy in copies:
            copy.start()

    pairs = ((normed_in, normed_t), (back_in, back_t), (two_in, two_t))
    loads = [pltpu.make_async_copy(src, flat.at[at], in_sem.at[at]) for at, (src, _) in enumerate(pairs)]
    start(loads)
    start(fetch(0, 0))

    if linked:
        chip, core, _, x_chip, y_chip, far_chip = position()
        x_dev, y_dev, other = (x_chip * 2 + core, z), (y_chip * 2 + core, z), (chip * 2 + 1 - core, z)
        half = pair.shape[2] // 2
        greet()
        shared = Share(packed, tokens_grad, *share_sems)
        shared.start()
        far = Far(tokens, weights, gains, biases, far_out, *far_scratch)
        far.start()

        def link(n, kind):
            sems = (send.at[n, kind], recv.at[n, kind])
            if kind == 0:
                return remote(staged.at[rem(n, 4), :, 1 - core], pair.at[n], *sems, other)
            if kind == 1:
                return remote(pair.at[n, far_chip, pl.ds(0, half)], x_half.at[n], *sems, x_dev)
            if kind == 2:
                return remote(pair.at[n, far_chip, pl.ds(half, half)], y_half.at[n], *sems, y_dev)
            if kind == 3:
                return remote(pair.at[n, x_chip], x_full.at[n], *sems, x_dev)
            return remote(pair.at[n, y_chip], y_full.at[n], *sems, y_dev)

        inner = rem(z, 2) + div(z, 2) == 1

        def z_link(n, kind):
            step = chunk(n)[1]
            step_there = step + 1 - 2 * rem(step, 2) if kind == 5 else tensors - 1 - step
            there = n + (step_there - step) * (1 + div(n + 4, 8))
            to = (chip * 2 + core, z_partner(z, 1 if kind == 5 else 3))
            return remote(
                pair.at[n, chip], z_sum.at[kind - 5, there], send.at[n, kind], recv.at[there, kind], to
            )

        def z_wait(n, kind):
            spot = z_sum.at[kind - 5, n]
            remote(spot, spot, send.at[n, kind], recv.at[n, kind], other).wait_recv()

        def add(ref, value):
            ref[...] = ref[...] + value

        def first(n):
            link(n, 0).wait_recv()
            link(n, 0).wait_send()
            slot = rem(n, 4)
            add(pair.at[n, far_chip], staged[slot, far_chip, core])
            link(n, 1).start()
            link(n, 2).start()
            for where in (x_chip, y_chip, chip):
                add(pair.at[n, where], staged[slot, where, core])

        def second(n):
            link(n, 1).wait_recv()
            add(pair.at[n, y_chip, pl.ds(0, half)], x_half[n])
            link(n, 4).start()
            link(n, 2).wait_recv()
            add(pair.at[n, x_chip, pl.ds(half, half)], y_half[n])
            link(n, 3).start()

        def third(n):
            link(n, 3).wait_recv()
            link(n, 4).wait_recv()
            mine = pair.at[n, chip]
            total = mine[...].astype(WIDE) + x_full[n].astype(WIDE) + y_full[n].astype(WIDE)
            mine[...] = total.astype(LOW)

            @pl.when(jnp.logical_and(chunk(n)[1] < tensors - 1, jnp.logical_not(inner)))
            def _():
                z_link(n, 5).start()

        def fourth(n):
            step = chunk(n)[1]

            @pl.when(jnp.logical_and(inner, step < 2))
            def _():
                z_wait(n, 5)
                add(pair.at[n, chip], z_sum[0, n])
                z_link(n, 6).start()

            @pl.when(jnp.logical_and(inner, step == 2))
            def _():
                z_wait(n, 6)
                add(pair.at[n, chip], z_sum[1, n])
                z_link(n, 5).start()

        def vec_link(step, kind):
            sems = (vec_send.at[step, kind], vec_recv.at[step, kind])
            t = z_partner(z, step)
            if kind == 0:
                return remote(vec_grads.at[t, :, 1 - core], vec_pair.at[step], *sems, other)
            if kind == 1:
                return remote(vec_pair.at[step, far_chip], vec_x.at[0, step], *sems, x_dev)
            if kind == 3:
                return remote(vec_pair.at[step, x_chip], vec_x.at[1, step], *sems, x_dev)
            if kind == 4:
                return remote(vec_pair.at[step, y_chip], vec_y.at[step], *sems, y_dev)
            return remote(vec_pair.at[step, chip], vec_z.at[step], *sems, (chip * 2 + core, t))

        steps = range(4)
        for step in steps:
            vec_link(step, 0).start()

        def vec_stage(stage):
            for step in steps:
                if stage == 0:
                    vec_link(step, 0).wait_recv()
                    vec_pair[step] += vec_grads[z_partner(z, step), :, core]
                    vec_link(step, 1).start()
                if stage == 1:
                    vec_link(step, 1).wait_recv()
                    add(vec_pair.at[step, y_chip], vec_x[0, step])
                    vec_link(step, 4).start()
                    vec_link(step, 3).start()
                if stage == 2:
                    vec_link(step, 3).wait_recv()
                    vec_link(step, 4).wait_recv()
                    add(vec_pair.at[step, chip], vec_x[1, step] + vec_y[step])
                    if step:
                        vec_link(step, 5).start()
                if stage == 3 and step:
                    vec_link(step, 5).wait_recv()
            if stage == 3:
                mine = vec_pair.at[0, chip]
                vec_out[...] = mine[...] + vec_z[1] + vec_z[2] + vec_z[3]
                for step in steps:
                    for kind in (0, 1, 3, 4, 5):
                        if kind < 5 or step:
                            vec_link(step, kind).wait_send()

    for load, (_, dst), at in zip(loads, pairs, range(3)):
        load.wait()
        dst[...] = flat[at].T
        if linked:
            vec_stage(at)

    def keep(n):
        group, step = chunk(n)
        return pltpu.make_async_copy(staged.at[rem(n, 4)], total_out.at[group, step], keep_sem.at[rem(n, 2)])

    def clear(n):
        if not linked:

            @pl.when(n > 1)
            def _():
                keep(n - 2).wait()

    shape = staged.shape[1:-1]

    @pl.loop(0, chunks + 6 if linked else chunks)
    def _(n):
        slot, place = rem(n, 2), rem(n, 4)
        paired = jnp.logical_and(n >= tensors, n < chunks)
        clear(n)

        @pl.when(n < tensors)
        def _():
            @pl.when(n + 1 < tensors)
            def _():
                start(fetch(n + 1, 0))

            @pl.when(n + 1 == tensors)
            def _():
                start(fetch(n + 1, 1))

            for copy in fetch(n, 0):
                copy.wait()
            wide = dot(normed_t[...], mixed_acts[slot]).astype(LOW)
            staged[place, :, :, :, : 3 * width] = wide.reshape(shape + (3 * width,))
            out = dot(back_t[...], attended_acts[slot]).astype(LOW)
            staged[place, :, :, :, 3 * width :] = out.reshape(shape + (width,))

        @pl.when(jnp.logical_and(paired, slot == 0))
        def _():
            start(fetch(n + 1, 2))
            for copy in fetch(n, 1):
                copy.wait()
            staged[place] = dot(two_t[...], acts[slot]).astype(LOW).reshape(shape + (hidden_width,))

        @pl.when(jnp.logical_and(paired, slot == 1))
        def _():
            @pl.when(n + 1 < chunks)
            def _():
                start(fetch(n + 1, 1))

            for copy in fetch(n, 2):
                copy.wait()

        if not linked:
            keep(n).start()
            return

        @pl.when(n < chunks)
        def _():
            link(n, 0).start()

        far.step(n - 1)
        for stage, lag in ((first, 1), (second, 2), (third, 3), (fourth, 6)):

            @pl.when(jnp.logical_and(n >= lag, n < chunks + lag))
            def _():
                stage(n - lag)

        for stage, step in enumerate((1, 3, 5, 7)):

            @pl.when(n == step)
            def _():
                shared.pass_on(stage)

    if linked:
        vec_stage(3)
        for group in range(3):
            n = max(n for n in range(chunks) if chunk(n)[0] == group)
            z_wait(n, 5)
            total_out[group] = pair[n, chip].astype(WIDE) + z_sum[0, n].astype(WIDE)

            @pl.when(inner)
            def _():
                z_wait(n, 6)
                total_out[group] += z_sum[1, n].astype(WIDE)

        @pl.loop(0, chunks)
        def _(n):
            for kind in range(1, 5):
                link(n, kind).wait_send()
            step = chunk(n)[1]

            @pl.when(jnp.logical_or(jnp.logical_and(step < tensors - 1, jnp.logical_not(inner)), jnp.logical_and(step == 2, inner)))
            def _():
                z_link(n, 5).wait_send()

            @pl.when(jnp.logical_and(step < 2, inner))
            def _():
                z_link(n, 6).wait_send()

        far.wait()
        shared.finish()
    else:
        keep(chunks - 2).wait()
        keep(chunks - 1).wait()


def weight_grads(
    packed, vec_grads, normed, two, back_low, qkv_back, attended, hidden_back, down_grads,
    tokens, weights, gains, biases, places, linked,
):
    tensors, rows, hidden_width = hidden_back.shape
    model = normed.shape[1]
    width = hidden_width // 4
    chunks = 3 * tensors
    dma = pltpu.SemaphoreType.DMA
    if linked:
        slab, chips = model // places, places // 2
        blocks = (chips, 2, slab, hidden_width)
        total = (3, slab, hidden_width), WIDE
        whole = (tensors,) + packed.shape
        vec_out = (8, 128)
        landing = [
            pltpu.VMEM((chunks, chips, slab, hidden_width), LOW),
            pltpu.VMEM((chunks, slab // 2, hidden_width), LOW),
            pltpu.VMEM((chunks, slab // 2, hidden_width), LOW),
            pltpu.VMEM((chunks, slab, hidden_width), LOW),
            pltpu.VMEM((chunks, slab, hidden_width), LOW),
            pltpu.VMEM((2, chunks, slab, hidden_width), LOW),
            pltpu.VMEM((4, chips, 8, 128), WIDE),
            pltpu.VMEM((2, 4, 8, 128), WIDE),
            pltpu.VMEM((4, 8, 128), WIDE),
            pltpu.VMEM((4, 8, 128), WIDE),
        ]
        vec_grads = vec_grads.reshape(tensors, chips, 2, 8, 128)
    else:
        blocks = (1, 1, model, hidden_width)
        total = (3, tensors) + blocks, LOW
        whole = vec_out = (8, 128)
        landing = [pltpu.VMEM((8, 128), WIDE)] * 10
    far_scratch = []
    if linked:
        padded = round_up(SEQ, ROWS)
        images = rows // padded - FAR_SENT
        far_rows, far_packed = images * padded, (round_up(images * SEQ, ROWS), model)
        far_scratch = [
            pltpu.VMEM((2,) + weights.shape[2:], LOW),
            pltpu.VMEM((images, padded + ROWS, model), LOW),
            pltpu.VMEM((far_rows, model), LOW),
            pltpu.VMEM((far_rows, model), LOW),
            pltpu.VMEM((far_rows, 3 * width), LOW),
            pltpu.VMEM((far_rows, width), LOW),
            pltpu.VMEM((far_rows, model), WIDE),
            pltpu.VMEM((far_rows, model), LOW),
            pltpu.VMEM((far_rows, hidden_width), WIDE),
            pltpu.VMEM((far_rows, hidden_width), LOW),
            pltpu.VMEM(far_packed, LOW),
            pltpu.VMEM((padded, padded), WIDE),
            pltpu.VMEM((padded, padded), LOW),
            pltpu.VMEM((images, 2, width, padded), LOW),
            dma((2,)),
            dma((images,)),
            dma,
        ]
    outs = ((whole, LOW), total, (vec_out, WIDE), (far_packed if linked else (8, 128), LOW))
    return pl.pallas_call(
        partial(grads_kernel, linked=linked),
        out_shape=[jax.ShapeDtypeStruct(shape, dtype) for shape, dtype in outs],
        in_specs=[ANY, VMEM] + [ANY] * 9 + [VMEM] * 2,
        out_specs=[ANY, VMEM if linked else ANY, VMEM, ANY],
        scratch_shapes=[pltpu.VMEM((3, rows, model), LOW)]
        + [pltpu.VMEM((model, rows), LOW)] * 3
        + [
            pltpu.VMEM((2, rows, hidden_width), LOW),
            pltpu.VMEM((2, rows, 3 * width), LOW),
            pltpu.VMEM((2, rows, width), LOW),
            pltpu.VMEM((4,) + blocks, LOW),
        ]
        + landing
        + [
            dma((3,)),
            dma((2, 2)),
            dma((2,)),
            dma((4, 6)),
            dma((4, 6)),
            dma((chunks, 7)),
            dma((chunks, 7)),
        ]
        + (share_scratch() if linked else [])
        + far_scratch,
        compiler_params=pltpu.CompilerParams(
            vmem_limit_bytes=58 * MEGA, has_side_effects=True, **({"collective_id": 2} if linked else {})
        ),
        name="weight_grads",
    )(
        packed, vec_grads, normed, two, back_low, qkv_back, attended, hidden_back, down_grads,
        tokens, weights, gains, biases,
    )


def adam_step(weight, gradient, first, second, rate, decay):
    first = BETA_ONE * first + (1.0 - BETA_ONE) * gradient
    second = BETA_TWO * second + (1.0 - BETA_TWO) * gradient * gradient
    corr_one = 1.0 - BETA_ONE**STEP
    corr_two = 1.0 - BETA_TWO**STEP
    updated = weight * (1.0 - rate * decay) - rate * (first / corr_one) / (
        jnp.sqrt(second / corr_two) + EPS_ADAM
    )
    return (first, second, updated)


def finish_kernel(*refs, linked, tensors, rows, slab, groups):
    refs = list(refs)
    wholes = [refs.pop(0) for _ in range(3)] if linked else []
    total, vec = refs.pop(0), refs.pop(0)
    inputs = [refs.pop(0) for _ in range(18)]
    flats = [refs.pop(0) for _ in range(2)] if linked else []
    outputs = [refs.pop(0) for _ in range(18)]
    held = [refs.pop(0) for _ in range(18)]
    news = [refs.pop(0) for _ in range(18)]
    small_in, small_out = refs.pop(0), refs.pop(0)
    params, moments = held[:6], held[6:]
    fetches = [pltpu.make_async_copy(inputs[at], held[at], small_in.at[at]) for at in range(18)]
    if linked:
        landed, far_landed, done, in_sem, out_sem, far_sem = refs

        far = far_block(lax.axis_index("tensor"), tensors)

        sent, far_rows = FAR_SENT * SEQ, rows - FAR_SENT * SEQ
        far_load = pltpu.make_async_copy(wholes[2], far_landed, far_sem)

        def load(at, t):
            return pltpu.make_async_copy(wholes[at].at[t], landed.at[at, t], in_sem.at[at, t])

        def store(at, t):
            begin, end = t * rows // ROWS * ROWS, (t + 1) * rows // ROWS * ROWS
            if t == tensors - 1:
                end = tensors * rows
            spot = pl.ds(begin, end - begin)
            return pltpu.make_async_copy(done.at[at, spot], flats[at].at[spot], out_sem.at[at, t])

        parts = [(at, t) for at in range(2) for t in range(tensors)]
        far_load.start()
        for part in parts:
            load(*part).start()
        for copy in fetches:
            copy.start()
        far_load.wait()
        for at, t in parts:
            load(at, t).wait()
            done[at, t * rows : (t + 1) * rows, :] = landed[at, t, :rows, :]
            if at == 0 and t in (0, tensors - 1):

                @pl.when(far == t)
                def _():
                    done[at, t * rows + sent : (t + 1) * rows, :] = far_landed[:far_rows, :]

            store(at, t).start()

    else:
        for copy in fetches:
            copy.start()

    width = total.shape[2] // 4

    for copy in fetches:
        copy.wait()

    def step(at, gradient, rate, decay, pick=()):
        weight, first, second = params[at], moments[2 * at], moments[2 * at + 1]
        values = adam_step(weight[pick], gradient, first[pick], second[pick], rate, decay)
        for out, value in zip(news[3 * at : 3 * at + 3], values):
            out[pick] = value

    for at in range(3):
        step(0, total[0, :, at * width : (at + 1) * width], RATE_MATRIX, DECAY_MATRIX, (at,))
    every = (slice(None),)
    step(1, total[0, :, 3 * width :].T, RATE_MATRIX, DECAY_MATRIX, every)
    step(2, total[1], RATE_MATRIX, DECAY_MATRIX, every)
    step(3, total[2], RATE_MATRIX, DECAY_MATRIX, every)
    step(4, vec[:6, :slab], RATE_VECTOR, 0.0, every)
    columns = vec[...].T
    shape = (columns.shape[0], 6 * groups)
    lane, row = (lax.broadcasted_iota(jnp.int32, shape, dim) for dim in (1, 0))
    attention = jnp.where(row < groups, 6 * row, jnp.where(row < 2 * groups, 6 * (row - groups) + 1, -1))
    hidden = jnp.where(row < 4 * groups, 6 * div(row, 4) + 2 + rem(row, 4), -1)
    picked = jnp.where(lane == attention, columns[:, 6:7], 0.0) + jnp.where(
        lane == hidden, columns[:, 7:8], 0.0
    )
    step(5, jnp.sum(picked, axis=0, keepdims=True), RATE_VECTOR, 0.0, every)
    stores = [pltpu.make_async_copy(news[at], outputs[at], small_out.at[at]) for at in range(18)]
    for copy in stores:
        copy.start()
    if linked:
        for part in parts:
            store(*part).wait()
    for copy in stores:
        copy.wait()


def finish(wholes, total, vec, params, moments, tensors, rows, slab, groups, linked):
    small = params + moments
    scratch = [pltpu.VMEM(value.shape, WIDE) for value in small]
    scratch += [pltpu.VMEM(param.shape, WIDE) for param in params for _ in range(3)]
    scratch += [pltpu.SemaphoreType.DMA((18,))] * 2
    outs, passed = [], ()
    if linked:
        passed = wholes
        model = wholes[0].shape[2]
        scratch += [
            pltpu.VMEM((2,) + wholes[0].shape, LOW),
            pltpu.VMEM(wholes[2].shape, LOW),
            pltpu.VMEM((2, tensors * rows, model), LOW),
            pltpu.SemaphoreType.DMA((2, tensors)),
            pltpu.SemaphoreType.DMA((2, tensors)),
            pltpu.SemaphoreType.DMA,
        ]
        outs = [jax.ShapeDtypeStruct((tensors * rows, model), LOW)] * 2
    news = [jax.ShapeDtypeStruct(param.shape, WIDE) for param in params for _ in range(3)]
    results = pl.pallas_call(
        partial(finish_kernel, linked=linked, tensors=tensors, rows=rows, slab=slab, groups=groups),
        out_shape=outs + news,
        in_specs=[ANY] * len(passed) + [VMEM] * 2 + [ANY] * 18,
        out_specs=[ANY] * (len(outs) + 18),
        scratch_shapes=scratch,
        compiler_params=pltpu.CompilerParams(vmem_limit_bytes=58 * MEGA),
        name="finish",
    )(*passed, total, vec, *small)
    if linked:
        return results[:2], list(results[2:])
    return wholes, list(results)


def own_parts(params, slab, width):
    qkv, out, up, down_t, shared, split = params
    mixed = jnp.concatenate([qkv[0], qkv[1], qkv[2], out.T], axis=1)
    table = split.reshape(-1, 6)
    rows = [shared, jnp.concatenate([table[:, 0], table[:, 1]])[None], table[:, 2:].reshape(1, -1)]
    vec = jnp.concatenate([jnp.pad(row, ((0, 0), (0, 128 - row.shape[1]))) for row in rows])
    return jnp.stack([mixed, up, down_t]).astype(LOW), vec


def per_device(
    tokens,
    cotangent,
    qkv_weight,
    out_weight,
    up_weight,
    down_weight,
    shared_vectors,
    split_vectors,
    qkv_first,
    qkv_second,
    out_first,
    out_second,
    up_first,
    up_second,
    down_first,
    down_second,
    shared_first,
    shared_second,
    split_first,
    split_second,
    *,
    places,
    tensors,
):
    linked = places == 8 and tensors == 4
    slab, width = qkv_weight.shape[1], qkv_weight.shape[2]
    model = slab * places
    groups = width // places
    rows = tokens.shape[0] // tensors
    images = rows // SEQ

    params = (qkv_weight, out_weight, up_weight, down_weight.T, shared_vectors, split_vectors)
    moments = (
        qkv_first, qkv_second, out_first, out_second, up_first, up_second,
        down_first.T, down_second.T, shared_first, shared_second, split_first, split_second,
    )
    sources = params
    if not linked:
        shard, vec = own_parts(params, slab, width)
        shard = lax.all_gather(lax.all_gather(shard, "dp", axis=1, tiled=True), "tensor", axis=1)
        vec = lax.all_gather(lax.all_gather(vec, "dp"), "tensor")
        sources = (shard, vec.reshape(tensors, places // 2, 2, 8, 128))
    packed, weights, own, back, back_t, gains, biases, *kept = forward(
        tokens, cotangent, sources, images, width, tensors, places, linked
    )
    normed, qkv, probs, attended, middle, two, hidden, slope = kept
    if not linked:
        weights = shard.reshape(3, tensors, 1, 1, model, 4 * width)
    packed_grad, block_out, hidden_back, back_low, qkv_back, vec_grads, down_grads = chain(
        packed, own, back, back_t, gains, weights, qkv, probs, middle, slope, hidden, places, linked
    )
    tokens_grad, total, vec_total, far = weight_grads(
        packed_grad, vec_grads, normed, two, back_low, qkv_back, attended, hidden_back, down_grads,
        tokens, weights, gains, biases, places, linked,
    )
    if linked:
        shares = (block_out, tokens_grad, far)
    else:
        shares = [lax.all_gather(part[:rows], "tensor", axis=0, tiled=True) for part in (packed, packed_grad)]
        total = total.reshape(3, tensors, model, 4 * width)
        total = lax.psum_scatter(total, "dp", scatter_dimension=2, tiled=True)
        total = lax.psum_scatter(total, "tensor", scatter_dimension=1).astype(WIDE)
        vec_total = lax.psum_scatter(vec_grads, "dp", scatter_dimension=1)
        vec_total = lax.psum_scatter(vec_total, "tensor", scatter_dimension=0)
    shares, news = finish(shares, total, vec_total, params, moments, tensors, rows, slab, groups, linked)
    news[9:12] = [new.T for new in news[9:12]]
    return (*shares, *news)


def solution(mesh):
    qkv, rows, cols = P(None, "dp", "tensor"), P("tensor", "dp"), P("dp", "tensor")
    shared, images = P(None, "dp"), P("dp", None)
    params = (qkv, rows, cols, rows, shared, rows)
    moments = tuple(spec for spec in params for _ in range(2))
    results = tuple(spec for spec in params for _ in range(3))
    return jax.shard_map(
        partial(per_device, places=mesh.shape["dp"], tensors=mesh.shape["tensor"]),
        mesh=mesh,
        in_specs=(images, images) + params + moments,
        out_specs=(images, images) + results,
        check_vma=False,
    )
```

time: 1060 us -> 258 us (0.24); the launches traced: 1050 us -> 258 us
  waiting for transfers between devices: 651 us -> 0 us
  Pallas kernels: 0 us -> 257 us
  matrix products: 165 us -> 0 us
  other arithmetic: 90.7 us -> 0 us
  local copies, waits for them, and re-layouts: 77.5 us -> 0 us
  blocking collectives: 46.1 us -> 0 us
  between operations: 17.4 us -> 0.86 us
    psum x3 -> x0, waiting for transfers between devices: 600 us -> none  [the longest x1 279 us: per_device(): lax.psum(feed_terms.astype(jnp.bfloat16), 'tensor').astype(jnp.float32)]
    pallas_call x0 -> x4, Pallas kernels: none -> 257 us  [the longest x1 103 us: weight_grads(): pl.pallas_call(partial(grads_kernel, linked=linked), out_shape=[jax.Shape...]
    dot_general x17 -> x0, matrix products: 159 us -> none  [the longest x3 36.4 us: contract_cols(): lax.dot_general(left, right, (((1,), (1,)), ((), ())), preferred_element_...]
    reduce_sum x11 -> x0, other arithmetic: 52.2 us -> none  [the longest x2 16.9 us: norm_backward(): jnp.sum(grad_out * unit, axis=0)]
    unnamed x15 -> x0, waiting for transfers between devices: 51.2 us -> none
    all_gather x3 -> x0, blocking collectives: 32.7 us -> none  [the longest x1 13.4 us: per_device(): lax.all_gather(qkv_weight.astype(low_type), 'dp', axis=1, tiled=True)]
    convert_element_type x6 -> x0, other arithmetic: 32.2 us -> none  [the longest x1 15.9 us: per_device(): grad_part = (middle_back + input_part).astype(low_type)]
    unnamed x144 -> x0, local copies, waits for them, and re-layouts: 26.2 us -> none
  transfers between devices with their start and end apart: 11 -> 0, of which waited for: 5 -> 0; matrix products, arithmetic and copies ran while one was open for 21% -> 0% of each run, Pallas kernels for 0% -> 0%
where the time goes in v1:
time: 258 us
  Pallas kernels  257 us (100%)
    pallas_call x1, Pallas kernels, weight_grads(): pl.pallas_call(partial(grads_kernel, linked=linked), out_shape=[jax.Shape...  103 us
    pallas_call x1, Pallas kernels, forward(): pl.pallas_call(partial(forward_kernel, linked=linked), out_shape=[jax.Sha...  81.7 us
    pallas_call x1, Pallas kernels, chain(): pl.pallas_call(partial(chain_kernel, linked=linked), out_shape=[jax.Shape...  61.5 us
    pallas_call x1, Pallas kernels, finish(): pl.pallas_call(partial(finish_kernel, linked=linked, tensors=tensors, row...  11.2 us

profile of v1, /device:TPU:0, one launch (start us, length us, event | category | flops | bytes accessed | tf_op | source)
XLA Modules:
  0.0 257.9 jit_solution(7762469929352847048)
XLA Ops:
  0.7 81.7 %forward.1 = (bf16[800,768]{1,0:T(8,128)(2,1)}, bf16[3,4,4,2,96,768]{5,4,3,2,1,0:T(8,128)(2,1)}, bf16[832,768]{1,0:T(8,128)(2,1)}, bf16[832,768]{1,0:T(8,128)(2,...) custom-call(bf16[3152,768]{1,0:T(8,128)(2,1)} %tokens.3, ...), custom_call_target="tpu_custom_call" | custom-call | tf_op jit(solution)/shard_map/forward/pallas_call | solution.py:701
  82.4 61.5 %chain.1 = (bf16[800,768]{1,0:T(8,128)(2,1)}, bf16[4,800,768]{2,1,0:T(8,128)(2,1)}, bf16[4,832,768]{2,1,0:T(8,128)(2,1)}, bf16[832,768]{1,0:T(8,128)(2,1)}, bf16...) custom-call(bf16[800,768]{1,0:T(8,128)(2,1)} %get-tuple-element.66.packed, ...), custom_call_target="tpu_custom_call" | custom-call | tf_op jit(solution)/shard_map/chain/pallas_call | solution.py:965
  143.9 102.6 %weight_grads.1 = (bf16[4,800,768]{2,1,0:T(8,128)(2,1)}, f32[3,96,768]{2,1,0:T(8,128)}, f32[8,128]{1,0:T(8,128)}, bf16[800,768]{1,0:T(8,128)(2,1)}) custom-call(bf16[800,768]{1,0:T(8,128)(2,1)} %get-tuple-element.78.packed, f32[4,4,2,8,128]{4,3,2,1,0:T(8,128)} %bitcast.11, bf16[832,768]{1,0:T(8,128)(2,1)} %get-tuple-element.80.normed_in, ...), custom_call_target="tpu_custom_call" | custom-call | tf_op jit(solution)/shard_map/weight_grads/pallas_call | solution.py:1475
  246.5 11.2 %finish.1 = (bf16[3152,768]{1,0:T(8,128)(2,1)}, bf16[3152,768]{1,0:T(8,128)(2,1)}, f32[3,96,192]{2,1,0:T(8,128)}, f32[3,96,192]{2,1,0:T(8,128)}, f32[3,96,192]{2...) custom-call(bf16[4,800,768]{2,1,0:T(8,128)(2,1)} %get-tuple-element., ...), custom_call_target="tpu_custom_call" | custom-call | tf_op jit(solution)/shard_map/finish/pallas_call | solution.py:1629

commit v2 on v1

--- a/solution.py
+++ b/solution.py
@@ -1104,25 +1104,28 @@
 
     def step(self, n):
         tensors = self.tensors
-
-        @pl.when(n == 0)
+        begin = tensors + 4
+
+        @pl.when(n == 1)
         def _():
             self.first_norm()
 
-        @pl.when(jnp.logical_and(n > 0, n <= tensors))
-        def _():
-            self.attention(n - 1)
-
-        @pl.when(n == tensors + 1)
+        @pl.when(jnp.logical_and(n > 1, n <= tensors + 1))
+        def _():
+            self.attention(n - 2)
+
+        @pl.when(n == tensors + 2)
         def _():
             self.second_norm()
 
-        @pl.when(jnp.logical_and(n > tensors + 1, n <= 2 * tensors + 1))
-        def _():
-            self.up(n - tensors - 2)
-            self.down(n - tensors - 2)
-
-        @pl.when(n == 2 * tensors + 2)
+        feeding = jnp.logical_and(n >= begin, n < begin + 2 * tensors)
+
+        @pl.when(jnp.logical_and(feeding, rem(n, 2) == 0))
+        def _():
+            self.up(div(n - begin, 2))
+            self.down(div(n - begin, 2))
+
+        @pl.when(n == begin + 2 * tensors - 1)
         def _():
             self.finish()
 
@@ -1368,7 +1371,7 @@
         def _():
             link(n, 0).start()
 
-        far.step(n - 1)
+        far.step(n)
         for stage, lag in ((first, 1), (second, 2), (third, 3), (fourth, 6)):
 
             @pl.when(jnp.logical_and(n >= lag, n < chunks + lag))

time: 258 us -> 259 us (level)
  no operation moved by 1% of the time
where the time goes in v2:
time: 259 us
  Pallas kernels  258 us (100%)
    pallas_call x1, Pallas kernels, weight_grads(): pl.pallas_call(partial(grads_kernel, linked=linked), out_shape=[jax.Shape...  104 us
    pallas_call x1, Pallas kernels, forward(): pl.pallas_call(partial(forward_kernel, linked=linked), out_shape=[jax.Sha...  81.7 us
    pallas_call x1, Pallas kernels, chain(): pl.pallas_call(partial(chain_kernel, linked=linked), out_shape=[jax.Shape...  61.5 us
    pallas_call x1, Pallas kernels, finish(): pl.pallas_call(partial(finish_kernel, linked=linked, tensors=tensors, row...  11.2 us

profile of v2, /device:TPU:0, one launch (start us, length us, event | category | flops | bytes accessed | tf_op | source)
XLA Modules:
  0.0 259.2 jit_solution(5857609678526663604)
XLA Ops:
  0.7 81.7 %forward.1 = (bf16[800,768]{1,0:T(8,128)(2,1)}, bf16[3,4,4,2,96,768]{5,4,3,2,1,0:T(8,128)(2,1)}, bf16[832,768]{1,0:T(8,128)(2,1)}, bf16[832,768]{1,0:T(8,128)(2,...) custom-call(bf16[3152,768]{1,0:T(8,128)(2,1)} %tokens.3, ...), custom_call_target="tpu_custom_call" | custom-call | tf_op jit(solution)/shard_map/forward/pallas_call | solution.py:701
  82.4 61.5 %chain.1 = (bf16[800,768]{1,0:T(8,128)(2,1)}, bf16[4,800,768]{2,1,0:T(8,128)(2,1)}, bf16[4,832,768]{2,1,0:T(8,128)(2,1)}, bf16[832,768]{1,0:T(8,128)(2,1)}, bf16...) custom-call(bf16[800,768]{1,0:T(8,128)(2,1)} %get-tuple-element.66.packed, ...), custom_call_target="tpu_custom_call" | custom-call | tf_op jit(solution)/shard_map/chain/pallas_call | solution.py:965
  143.9 103.9 %weight_grads.1 = (bf16[4,800,768]{2,1,0:T(8,128)(2,1)}, f32[3,96,768]{2,1,0:T(8,128)}, f32[8,128]{1,0:T(8,128)}, bf16[800,768]{1,0:T(8,128)(2,1)}) custom-call(bf16[800,768]{1,0:T(8,128)(2,1)} %get-tuple-element.78.packed, f32[4,4,2,8,128]{4,3,2,1,0:T(8,128)} %bitcast.11, bf16[832,768]{1,0:T(8,128)(2,1)} %get-tuple-element.80.normed_in, ...), custom_call_target="tpu_custom_call" | custom-call | tf_op jit(solution)/shard_map/weight_grads/pallas_call | solution.py:1478
  247.8 11.2 %finish.1 = (bf16[3152,768]{1,0:T(8,128)(2,1)}, bf16[3152,768]{1,0:T(8,128)(2,1)}, f32[3,96,192]{2,1,0:T(8,128)}, f32[3,96,192]{2,1,0:T(8,128)}, f32[3,96,192]{2...) custom-call(bf16[4,800,768]{2,1,0:T(8,128)(2,1)} %get-tuple-element., ...), custom_call_target="tpu_custom_call" | custom-call | tf_op jit(solution)/shard_map/finish/pallas_call | solution.py:1632
